TPU v7x, 512 devices: a whole 4x4x16 slice. The times are simulated.
512 devices in a mesh: pts: 128 (over y, z, core), grp: 4 (over x).
Axes of the slice: x: 4, y: 4, z: 16, core: 2. Of those that a mesh axis runs over, the one named last changes fastest.
Arguments:
- features: bfloat16 [4, 65536, 256], P('grp', 'pts'), may hold values from -6 to 6
- hilbert_slot: int32 [4, 65536], P('grp', 'pts'), may hold values from 0 to 524287, as said below
- hilbert_count: int32 [4, 128], P('grp', 'pts'), may hold values from 256 to 1024, as said below
- norm_gain: float32 [2, 2, 256], replicated, may hold values from 0.1 to 1.9
- norm_shift: float32 [2, 2, 256], replicated, may hold values from -3 to 3
- qkv_weight: bfloat16 [2, 256, 768], replicated, may hold values from -0.75 to 0.75
- proj_weight: bfloat16 [2, 256, 256], replicated, may hold values from -0.375 to 0.375
- up_weight: bfloat16 [2, 256, 1024], replicated, may hold values from -0.375 to 0.375
- up_bias: float32 [2, 1024], replicated, may hold values from -3 to 3
- down_weight: bfloat16 [2, 1024, 256], replicated, may hold values from -0.1875 to 0.1875
- out_bias: float32 [2, 2, 256], replicated, may hold values from -3 to 3
Outputs:
- refined: bfloat16 [4, 65536, 256], P('grp', 'pts')
Inputs may be any that keep to these rules, and one draw needn't show every extreme that they name: hilbert_slot = (owner group * 128 + owner index) * 1024 + position; every slot is used at most once and each owner's used positions are exactly those below its hilbert_count. The owner's group is the point's own, except that positions below 64 of index 0 of every group hold points of the previous group (the last group's go to group 0). Counting points for index 0 of the own group together with those that go on to the next group, no device sends more than 16 points to one index of its group, and some device sends exactly 16; every device sends exactly 16 points to each aligned four indices of its group. The last owner of the last group holds 1024 points. `hilbert_count`: in each aligned four owners of a group, one holds 1024 points and the four hold 2048 together.
All inputs are finite; a program needn't handle non-finite values.
Results may differ from a plain program's by a relative error of at most 0.034.
Values may be sent and summed in bfloat16 or wider, within the bound.
A program may use at most 64 MiB of HBM per device.

v0:
```python
import jax
import jax.numpy as jnp
from jax import lax
from jax.sharding import PartitionSpec as P

HEADS = 16
BOUND = 64


NORM_EPS = 1e-05


def swapped(shard, axis, distance):
    return lax.ppermute(shard, axis, [(i, i ^ 1 << distance) for i in range(lax.axis_size(axis))])


def shifted(value, axis, steps):
    count = lax.axis_size(axis)
    pairs = [(source, (source + steps) % count) for source in range(count)]
    return lax.ppermute(value, axis, pairs)


def layer_norm(input_rows, norm_scale, norm_offset):
    input_rows = input_rows.astype(jnp.float32)
    center = jnp.mean(input_rows, axis=-1, keepdims=True)
    centered = input_rows - center
    spread = jnp.mean(centered * centered, axis=-1, keepdims=True)
    return centered * lax.rsqrt(spread + NORM_EPS) * norm_scale + norm_offset


def project_columns(normed, matrix):
    return jnp.einsum("rd,de->er", normed, matrix, preferred_element_type=jnp.float32).astype(
        jnp.bfloat16
    )


def head_attention(queries, keys_all, values_all, live_mask, score_scale):

    def one_head(pieces):
        q_one, k_one, v_one = pieces
        scores = (
            jnp.einsum("dq,dk->qk", q_one, k_one, preferred_element_type=jnp.float32) * score_scale
        )
        exp_scores = jnp.where(live_mask[None, :], jnp.exp(scores), 0.0)
        denominator = jnp.sum(exp_scores, axis=1)
        weights_low = exp_scores.astype(jnp.bfloat16)
        attended = jnp.einsum("dk,qk->dq", v_one, weights_low, preferred_element_type=jnp.float32)
        return (attended / denominator[None, :]).astype(jnp.bfloat16)

    return lax.map(one_head, (queries, keys_all, values_all))


def finish_attention(input_rows, attended, proj_matrix, proj_offset):
    merged = attended.reshape(-1, attended.shape[-1])
    projected_out = (
        jnp.einsum("dq,de->qe", merged, proj_matrix, preferred_element_type=jnp.float32)
        + proj_offset
    )
    return (input_rows.astype(jnp.float32) + projected_out).astype(jnp.bfloat16)


def feed_forward(
    input_rows, norm_scale, norm_offset, up_matrix, up_offset, down_matrix, down_offset
):
    normed = layer_norm(input_rows, norm_scale, norm_offset).astype(jnp.bfloat16)
    pre_act = jnp.dot(normed, up_matrix, preferred_element_type=jnp.float32) + up_offset
    hidden = jax.nn.gelu(pre_act, approximate=False).astype(jnp.bfloat16)
    projected_out = jnp.dot(hidden, down_matrix, preferred_element_type=jnp.float32) + down_offset
    return (input_rows.astype(jnp.float32) + projected_out).astype(jnp.bfloat16)


def split_heads(columns, head_dim):
    return columns.reshape(HEADS, head_dim, columns.shape[-1])


def bucket_ranks(target_ids, bucket_count):
    onehot = (target_ids[:, None] == jnp.arange(bucket_count, dtype=jnp.int32)[None, :]).astype(
        jnp.int32
    )
    return jnp.sum(jnp.cumsum(onehot, axis=0) * onehot, axis=1) - 1


def on_device(
    features,
    hilbert_slot,
    hilbert_count,
    norm_gain,
    norm_shift,
    qkv_weight,
    proj_weight,
    up_weight,
    up_bias,
    down_weight,
    out_bias,
):
    local_rows = features[0]
    rows_count = local_rows.shape[0]
    feature_width = local_rows.shape[1]
    head_dim = feature_width // HEADS
    score_scale = head_dim ** (-0.5)
    patch_size = 2 * rows_count
    owner_count = lax.axis_size("pts")
    pair_slots = 4 * rows_count // owner_count
    normed = layer_norm(local_rows, norm_gain[0, 0], norm_shift[0, 0]).astype(jnp.bfloat16)
    projected = project_columns(normed, qkv_weight[0])
    partner = swapped(projected[feature_width:], "pts", 0)
    key_value = jnp.concatenate([projected[feature_width:], partner], axis=1)
    all_live = jnp.ones((2 * rows_count,), jnp.bool_)
    attended = head_attention(
        split_heads(projected[:feature_width], head_dim),
        split_heads(key_value[:feature_width], head_dim),
        split_heads(key_value[feature_width:], head_dim),
        all_live,
        score_scale,
    )
    mixed_one = finish_attention(local_rows, attended, proj_weight[0], out_bias[0, 0])
    after_one = feed_forward(
        mixed_one,
        norm_gain[0, 1],
        norm_shift[0, 1],
        up_weight[0],
        up_bias[0],
        down_weight[0],
        out_bias[0, 1],
    )
    group_index = lax.axis_index("grp")
    slot_ids = hilbert_slot[0]
    owner_global = slot_ids // patch_size
    target = owner_global % owner_count
    position = slot_ids % patch_size
    onward = owner_global // owner_count != group_index
    target_slot = jnp.where(onward, 0, target)
    slot_tag = position + patch_size * onward.astype(jnp.int32)
    bucket_rank = bucket_ranks(target_slot, owner_count)
    send_rows = (
        jnp.zeros((owner_count, pair_slots, feature_width), jnp.bfloat16)
        .at[target_slot, bucket_rank]
        .set(after_one)
    )
    send_tags = (
        jnp.full((owner_count, pair_slots), -1, jnp.int32)
        .at[target_slot, bucket_rank]
        .set(slot_tag)
    )
    recv_rows, recv_tags = (
        lax.all_to_all(send_rows, "pts", split_axis=0, concat_axis=0, tiled=True),
        lax.all_to_all(send_tags, "pts", split_axis=0, concat_axis=0, tiled=True),
    )
    flat_rows = recv_rows.reshape(owner_count * pair_slots, feature_width)
    flat_tags = recv_tags.reshape(owner_count * pair_slots)
    held = flat_tags >= 0
    local_tags = jnp.where(held, flat_tags, 0)
    onward_in = held & (local_tags >= patch_size)
    local_index = jnp.where(held & (local_tags < patch_size), local_tags, patch_size)
    owner_rows = (
        jnp.zeros((patch_size, feature_width), jnp.bfloat16)
        .at[local_index]
        .set(flat_rows, mode="drop")
    )
    relay_index = jnp.where(onward_in, local_tags - patch_size, BOUND)
    relayed = (
        jnp.zeros((BOUND, feature_width), jnp.bfloat16).at[relay_index].set(flat_rows, mode="drop")
    )
    arrived = shifted(relayed, "grp", 1)
    owner_rows = jnp.concatenate([owner_rows[:BOUND] + arrived, owner_rows[BOUND:]], axis=0)
    live_mask = jnp.arange(patch_size, dtype=jnp.int32) < hilbert_count[0, 0]
    normed_two = layer_norm(owner_rows, norm_gain[1, 0], norm_shift[1, 0]).astype(jnp.bfloat16)
    projected_two = project_columns(normed_two, qkv_weight[1])
    attended_two = head_attention(
        split_heads(projected_two[:feature_width], head_dim),
        split_heads(projected_two[feature_width : 2 * feature_width], head_dim),
        split_heads(projected_two[2 * feature_width :], head_dim),
        live_mask,
        score_scale,
    )
    mixed_two = finish_attention(owner_rows, attended_two, proj_weight[1], out_bias[1, 0])
    leaving = feed_forward(
        mixed_two,
        norm_gain[1, 1],
        norm_shift[1, 1],
        up_weight[1],
        up_bias[1],
        down_weight[1],
        out_bias[1, 1],
    )
    back_rows = shifted(leaving[:BOUND], "grp", -1)
    reply_table = jnp.concatenate([leaving, back_rows], axis=0)
    reply_rows = reply_table[local_tags].reshape(owner_count, pair_slots, feature_width)
    returned = lax.all_to_all(reply_rows, "pts", split_axis=0, concat_axis=0, tiled=True)
    home_rows = returned[target_slot, bucket_rank]
    return home_rows[None]


def solution(mesh):
    return jax.shard_map(
        on_device,
        mesh=mesh,
        in_specs=(
            P("grp", "pts", None),
            P("grp", "pts"),
            P("grp", "pts"),
            P(),
            P(),
            P(),
            P(),
            P(),
            P(),
            P(),
            P(),
        ),
        out_specs=P("grp", "pts", None),
        check_vma=False,
    )
```

profile of v0, /device:TPU:1, one launch (start us, length us, event | category | flops | bytes accessed | tf_op | source)
XLA Modules:
  0.0 370.2 jit_solution(5481860864191009964)
XLA Ops:
  0.0 1.1 copy.30
  1.3 0.8 fusion.260
  2.1 0.8 fusion.261
  2.8 1.5 fusion.68
  4.4 8.8 %collective-permute-start = (bf16[512,512]{0,1:T(8,128)(2,1)S(1)}, bf16[512,512]{0,1:T(8,128)(2,1)S(1)}, u32[]{:S(2)}, u32[]{:S(2)}) collective-permute-start(bf16[512,512]{0,1:T(8,128)(2,1)S(1)} %slice.146), channel_id=1, source_target_pairs={{0,4},{4,0},{8,12},{12,8},{16,20},{20,16},{24,28},{28,24},{32,36},... | collective-permute-start | bytes 1572872 | tf_op jit(solution)/shard_map/ppermute | solution.py:14
  14.0 24.6 %scatter_fusion = s32[128,16]{0,1:T(8,128)S(1)} fusion(s32[128,16]{0,1:T(8,128)S(1)} %broadcast_in_dim.54, s32[512]{0:T(512)S(1)} %bitcast.157, s32[512]{0:T(512)S(1)} %get-tuple-element.108), kind=kCustom, calls=%fused_computation.2 | custom fusion | bytes 10240 | tf_op jit(solution)/shard_map/scatter | solution.py:143
  38.6 0.7 copy.29
  39.3 14.4 %all-to-all-start = ((s32[128,1,16]{2,1,0:T(1,128)}), s32[128,1,16]{2,1,0:T(1,128)S(1)}, u32[]{:S(2)}, u32[]{:S(2)}) async-start(s32[128,1,16]{2,1,0:T(1,128)} %copy.29), calls=%async_computation | async-start | bytes 131072 | tf_op jit(solution)/shard_map/all_to_all | solution.py:147
  54.5 15.4 %while.21 = (s32[]{:T(128)}, bf16[16,16,512]{2,1,0:T(8,128)(2,1)S(1)}, bf16[16,16,1024]{2,1,0:T(8,128)(2,1)S(1)}, bf16[16,16,512]{2,1,0:T(8,128)(2,1)S(1)}, bf16[16,16,1024]{2,1,0:T(8,128)(2,1)S(1)}, /*index=5*/s32[]{:T(128)}) while((s32[]{:T(128)}, bf16[16,16,512]{2,1,0:T(8,128)(2,1)S(1)}, bf16[16,16,1024]{2,1,0:T(8,128)(2,1)S(1)}, ...), condition=%wide.region_8.9_spmd, body=%wide.region_6.8_spmd.sunk | while | flops 35667456 | bytes 4298821 | solution.py:50
  70.3 6.4 %fusion.79 = bf16[512,256]{0,1:T(8,128)(2,1)S(1)} fusion(f32[512,256]{0,1:T(8,128)S(1)} %get-tuple-element.142, f32[1024]{0:T(1024)S(1)} %bitcast.181, bf16[2,1024,256]{2,1,0:T(8,128)(2,1)S(1)} %copy-done.4, bf16[2,256,1024]{2,1,0:T(8,128)(2,1)} %param.22, f32[256]{0:T(256)S(1)} %bitcast.191, f32[256]{0:T(256)S(1)} %bitcast.190, f32[256]{0:T(256)S(1)} %bitcast.189, ...), kind=kOutput, calls=%fused_computation.108 | convolution fusion | flops 572522496 | bytes 2370560 | tf_op jit(solution)/shard_map/dot_general | solution.py:68
  76.9 1.1 broadcast_in_dim.55
  77.9 55.5 %scatter_fusion.1 = bf16[128,16,256]{2,1,0:T(8,128)(2,1)} fusion(bf16[128,16,256]{2,1,0:T(8,128)(2,1)} %broadcast_in_dim.55, s32[512]{0:T(512)S(1)} %bitcast.158, bf16[512,256]{1,0:T(8,128)(2,1)S(1)} %copy.35), kind=kCustom, calls=%fused_computation.3 | custom fusion | bytes 790528 | tf_op jit(solution)/shard_map/scatter | solution.py:138
  133.4 16.5 %all-to-all-start.1 = ((bf16[128,16,256]{2,1,0:T(8,128)(2,1)}), bf16[128,16,256]{2,1,0:T(8,128)(2,1)S(1)}, u32[]{:S(2)}, u32[]{:S(2)}) async-start(bf16[128,16,256]{2,1,0:T(8,128)(2,1)} %scatter_fusion.1), calls=%async_computation.1 | async-start | bytes 2097152 | tf_op jit(solution)/shard_map/all_to_all | solution.py:146
  150.4 0.8 reduce.4
  151.4 52.8 %all-to-all-done.1 = bf16[128,16,256]{2,1,0:T(8,128)(2,1)S(1)} async-done(((bf16[128,16,256]{2,1,0:T(8,128)(2,1)}), bf16[128,16,256]{2,1,0:T(8,128)(2,1)S(1)}, u32[]{:S(2)}, u32[]{:S(2)}) %all-to-all-start.1) | async-done | bytes 1048608 | tf_op jit(solution)/shard_map/all_to_all | solution.py:146
  204.2 9.2 %scatter_custom_fusion.3 = bf16[64,256]{1,0:T(8,128)(2,1)S(1)} fusion(s32[2048]{0:T(1024)S(1)} %bitcast.179, bf16[2048,256]{1,0:T(8,128)(2,1)S(1)} %bitcast.162, bf16[]{:T(256)} %constant.67.clone.1), kind=kCustom, calls=%fused_computation.216 | custom fusion | bytes 32770 | tf_op jit(solution)/shard_map/scatter | solution.py:162
  213.4 3.4 collective-permute-start.1
  216.8 9.4 %scatter_custom_fusion.2 = bf16[1024,256]{1,0:T(8,128)(2,1)S(1)} fusion(s32[2048]{0:T(1024)S(1)} %bitcast.178, bf16[2048,256]{1,0:T(8,128)(2,1)S(1)} %bitcast.163, bf16[]{:T(256)} %constant.67.clone.1), kind=kCustom, calls=%fused_computation.201 | custom fusion | bytes 524290 | tf_op jit(solution)/shard_map/scatter | solution.py:158
  227.3 0.9 fusion.67
  228.4 47.8 %while.22 = (s32[]{:T(128)}, bf16[16,16,1024]{2,1,0:T(8,128)(2,1)}, bf16[16,16,1024]{2,1,0:T(8,128)(2,1)S(1)}, bf16[16,16,1024]{2,1,0:T(8,128)(2,1)S(1)}, bf16[1...) while((s32[]{:T(128)}, bf16[16,16,1024]{2,1,0:T(8,128)(2,1)}, ...), condition=%wide.region_18.19_spmd.clone, body=%wide.region_16.18_spmd.clone.sunk | while | flops 73433088 | bytes 8533073 | solution.py:50
  228.4 0.7 iota_compare_fusion.5
  229.0 1.0 fusion.280
  230.0 1.3 fusion.281
  231.3 0.6 iota_compare_fusion.5
  232.0 1.0 fusion.280
  233.0 1.3 fusion.281
  235.0 1.0 fusion.280
  236.0 1.3 fusion.281
  237.3 0.6 iota_compare_fusion.5
  237.9 1.0 fusion.280
  239.0 1.3 fusion.281
  240.3 0.6 iota_compare_fusion.5
  240.9 1.0 fusion.280
  241.9 1.3 fusion.281
  243.9 1.0 fusion.280
  244.9 1.3 fusion.281
  246.9 1.0 fusion.280
  247.9 1.3 fusion.281
  249.9 1.0 fusion.280
  250.9 1.3 fusion.281
  252.2 0.6 iota_compare_fusion.5
  252.8 1.0 fusion.280
  253.8 1.3 fusion.281
  255.8 1.0 fusion.280
  256.8 1.3 fusion.281
  258.8 1.0 fusion.280
  259.8 1.3 fusion.281
  261.8 1.0 fusion.280
  262.8 1.3 fusion.281
  264.7 1.0 fusion.280
  265.8 1.3 fusion.281
  267.7 1.0 fusion.280
  268.7 1.3 fusion.281
  270.7 1.0 fusion.280
  271.7 1.3 fusion.281
  273.7 1.0 fusion.280
  274.7 1.3 fusion.281
  276.2 1.6 convert_reduce_fusion
  278.2 10.0 %fusion.70 = bf16[1024,256]{1,0:T(8,128)(2,1)S(1)} fusion(bf16[1024,256]{1,0:T(8,128)(2,1)S(1)} %get-tuple-element.144, f32[1024]{0:T(1024)S(1)} %bitcast.180, f32[256]{0:T(256)S(1)} %bitcast.187, bf16[2,1024,256]{2,1,0:T(8,128)(2,1)S(1)} %copy-done.4, bf16[2,256,1024]{2,1,0:T(8,128)(2,1)S(1)} %copy-done.5, f32[256]{0:T(256)S(1)} %bitcast.184, ...), kind=kOutput, calls=%fused_computation.97 | convolution fusion | flops 1145569280 | bytes 2636800 | tf_op jit(solution)/shard_map/dot_general | solution.py:68
  288.2 3.1 collective-permute-start.2
  291.3 1.6 collective-permute-done.2
  292.9 7.5 %gather_fusion = bf16[2048,256]{1,0:T(8,128)(2,1)S(1)} fusion(bf16[1088,256]{1,0:T(8,128)(2,1)S(1)} %pad_maximum_fusion, s32[2048]{0:T(1024)S(1)} %broadcast_clamp_fusion), kind=kCustom, calls=%fused_computation | custom fusion | bytes 2105344 | tf_op jit(solution)/shard_map/gather | solution.py:188
  300.4 64.0 %all_to_all.19 = bf16[128,16,256]{2,1,0:T(8,128)(2,1)S(1)} all-to-all(bf16[128,16,256]{2,1,0:T(8,128)(2,1)S(1)} %bitcast.160), channel_id=1, replica_groups=mesh['pts'=128,'grp'=4] {'pts'}, dimensions={0} | all-to-all | bytes 2097152 | tf_op jit(solution)/shard_map/all_to_all | solution.py:189
  364.4 5.6 %gather_fusion.1 = bf16[512,256]{1,0:T(8,128)(2,1)} fusion(bf16[128,16,256]{2,1,0:T(8,128)(2,1)S(1)} %all_to_all.19, s32[512]{0:T(512)S(1)} %bitcast.159), kind=kCustom, calls=%fused_computation.1 | custom fusion | bytes 528384 | tf_op jit(solution)/shard_map/gather | solution.py:190
  (110 shorter events, 26.9 us)
Async XLA Ops:
  0.0 13.2 %copy-start.1 = (s32[1,512]{1,0:T(1,128)S(1)}, s32[1,512]{1,0:T(1,128)}, u32[]{:S(2)}) copy-start(s32[1,512]{1,0:T(1,128)} %param.16) | copy-start | bytes 6148
  4.4 49.6 %collective-permute-start = (bf16[512,512]{0,1:T(8,128)(2,1)S(1)}, bf16[512,512]{0,1:T(8,128)(2,1)S(1)}, u32[]{:S(2)}, u32[]{:S(2)}) collective-permute-start(bf16[512,512]{0,1:T(8,128)(2,1)S(1)} %slice.146), channel_id=1, source_target_pairs={{0,4},{4,0},{8,12},{12,8},{16,20},{20,16},{24,28},{28,24},{32,36},... | collective-permute-start | bytes 1572872 | tf_op jit(solution)/shard_map/ppermute | solution.py:14
  14.0 39.9 %copy-start.3 = (f32[2,2,256]{2,1,0:T(2,128)S(1)}, f32[2,2,256]{2,1,0:T(2,128)}, u32[]{:S(2)}) copy-start(f32[2,2,256]{2,1,0:T(2,128)} %param.25) | copy-start | bytes 12292
  14.0 39.9 %copy-start.2 = (f32[2,1024]{1,0:T(2,128)S(1)}, f32[2,1024]{1,0:T(2,128)}, u32[]{:S(2)}) copy-start(f32[2,1024]{1,0:T(2,128)} %param.23) | copy-start | bytes 24580
  39.3 94.1 %all-to-all-start = ((s32[128,1,16]{2,1,0:T(1,128)}), s32[128,1,16]{2,1,0:T(1,128)S(1)}, u32[]{:S(2)}, u32[]{:S(2)}) async-start(s32[128,1,16]{2,1,0:T(1,128)} %copy.29), calls=%async_computation | async-start | bytes 131072 | tf_op jit(solution)/shard_map/all_to_all | solution.py:147
  54.5 15.4 %copy-start = (bf16[2,256,256]{2,1,0:T(8,128)(2,1)S(1)}, bf16[2,256,256]{2,1,0:T(8,128)(2,1)}, u32[]{:S(2)}) copy-start(bf16[2,256,256]{2,1,0:T(8,128)(2,1)} %param.21) | copy-start | bytes 786436
  54.5 15.8 %copy-start.4 = (bf16[2,1024,256]{2,1,0:T(8,128)(2,1)S(1)}, bf16[2,1024,256]{2,1,0:T(8,128)(2,1)}, u32[]{:S(2)}) copy-start(bf16[2,1024,256]{2,1,0:T(8,128)(2,1)} %param.24) | copy-start | bytes 3145732
  133.4 70.8 %all-to-all-start.1 = ((bf16[128,16,256]{2,1,0:T(8,128)(2,1)}), bf16[128,16,256]{2,1,0:T(8,128)(2,1)S(1)}, u32[]{:S(2)}, u32[]{:S(2)}) async-start(bf16[128,16,256]{2,1,0:T(8,128)(2,1)} %scatter_fusion.1), calls=%async_computation.1 | async-start | bytes 2097152 | tf_op jit(solution)/shard_map/all_to_all | solution.py:146
  213.4 12.9 %collective-permute-start.1 = (bf16[64,256]{1,0:T(8,128)(2,1)S(1)}, bf16[64,256]{1,0:T(8,128)(2,1)S(1)}, u32[]{:S(2)}, u32[]{:S(2)}) collective-permute-start(bf16[64,256]{1,0:T(8,128)(2,1)S(1)} %scatter_custom_fusion.3), channel_id=1, source_target_pairs={{0,1},{1,2},{2,3},{3,0},{4,5},{5,6},{6,7},{7,4},{8,9},{9,10},{10,1... | collective-permute-start | bytes 98312 | tf_op jit(solution)/shard_map/ppermute | solution.py:20
  226.2 1.1 copy-start.6
  276.2 2.0 copy-start.5
  288.2 4.7 %collective-permute-start.2 = (bf16[64,256]{1,0:T(8,128)(2,1)S(1)}, bf16[64,256]{1,0:T(8,128)(2,1)S(1)}, u32[]{:S(2)}, u32[]{:S(2)}) collective-permute-start(bf16[64,256]{1,0:T(8,128)(2,1)S(1)} %slice.155), channel_id=1, source_target_pairs={{0,3},{1,0},{2,1},{3,2},{4,7},{5,4},{6,5},{7,6},{8,11},{9,8},{10,9... | collective-permute-start | bytes 98312 | tf_op jit(solution)/shard_map/ppermute | solution.py:20
where the time goes:
time: 376 us; the launch traced here: 370 us
  local copies, waits for them, and re-layouts  118 us (31%)
  matrix products  73.1 us (19%)
  blocking collectives  64 us (17%)
  waiting for transfers between devices  54.4 us (14%)
  starting transfers between devices  46.1 us (12%)
  other arithmetic  13.2 us (4%)
    all_to_all x1, blocking collectives, on_device(): lax.all_to_all(reply_rows, 'pts', split_axis=0, concat_axis=0, tiled=True)  64 us
    scatter x1, local copies, waits for them, and re-layouts, on_device(): send_rows = jnp.zeros((owner_count, pair_slots, feature_width), jnp.bfloa...  55.5 us
    all_to_all x1, waiting for transfers between devices, on_device(): lax.all_to_all(send_rows, 'pts', split_axis=0, concat_axis=0, tiled=True)  52.8 us
    dot_general x32, matrix products, one_head(): jnp.einsum('dk,qk->dq', v_one, weights_low, preferred_element_type=jnp.fl...  27.3 us
    dot_general x32, matrix products, one_head(): jnp.einsum('dq,dk->qk', q_one, k_one, preferred_element_type=jnp.float32)  25 us
    scatter x1, local copies, waits for them, and re-layouts, on_device(): send_tags = jnp.full((owner_count, pair_slots), -1, jnp.int32).at[target_...  24.6 us
    all_to_all x1, starting transfers between devices, on_device(): lax.all_to_all(send_rows, 'pts', split_axis=0, concat_axis=0, tiled=True)  16.5 us
    dot_general x2, matrix products, feed_forward(): jnp.dot(hidden, down_matrix, preferred_element_type=jnp.float32)  16.4 us
  transfers between devices with their start and end apart: 5, of which 2 were waited for; matrix products, arithmetic and copies ran while one was open for 31% of the time, Pallas kernels for 0%

commit v1 on v0

v1 whole, which is shorter than its diff:
```python
import functools

import jax
import jax.numpy as jnp
from jax import lax
from jax.experimental import pallas as pl
from jax.experimental.pallas import tpu as pltpu
from jax.sharding import PartitionSpec as P

BF = jnp.bfloat16
F32 = jnp.float32
I32 = jnp.int32
MESH = pl.DeviceIdType.MESH
NORM_EPS = 1e-05
SCALE = 0.25 * 1.4426950408889634
ROWS = 512
WIDTH = 256
PATCH = 1024
CROSS = 64
PEERS = 48


def layer_norm(rows, gain, shift):
    rows = rows.astype(F32)
    centered = rows - jnp.mean(rows, axis=-1, keepdims=True)
    spread = jnp.mean(centered * centered, axis=-1, keepdims=True)
    return (centered * lax.rsqrt(spread + NORM_EPS) * gain + shift).astype(BF)


def mm(left, right):
    return jnp.dot(left, right, preferred_element_type=F32)


def mm_nt(left, right):
    return lax.dot_general(left, right, (((1,), (1,)), ((), ())), preferred_element_type=F32)


def iota(shape, dim):
    return lax.broadcasted_iota(I32, shape, dim)


def onehot(mask):
    return jnp.where(mask, 1.0, 0.0).astype(BF)


def gelu(values):
    return 0.5 * values * (1.0 + lax.erf(values * 0.7071067811865476))


def pipelined(parts, score, finish):
    scores = score(parts[0])
    for index, part in enumerate(parts):
        ahead = score(parts[index + 1]) if index + 1 < len(parts) else None
        finish(part, scores)
        scores = ahead


def kernel(
    x_ref,
    slot_ref,
    gain_ref,
    shift_ref,
    qkv_ref,
    proj_ref,
    up_ref,
    upb_ref,
    down_ref,
    outb_ref,
    out_ref,
    px,
    xp,
    qbuf,
    kbuf,
    vobuf,
    send_a,
    recv_a,
    tag_send,
    tag_recv,
    tag_quad,
    zrows,
    gath,
    dsend,
    sort_m,
    unsort_m,
    home_m,
    gs,
    kpack,
    cross_out,
    cross_in,
    att_s,
    catt_out,
    catt_in,
    zatt_out,
    zatt_in,
    own_att,
    datt_out,
    datt_in,
    ret_send,
    home,
    ab_send,
    ab_recv,
    tag_ssem,
    tag_rsem,
    quad_ssem,
    quad_rsem,
    pair_sem,
    z_ssem,
    z_rsem,
    d_ssem,
    d_rsem,
    cross_sem,
    catt_sem,
    za_ssem,
    za_rsem,
    da_ssem,
    da_rsem,
    rt_ssem,
    rt_rsem,
):
    me = lax.axis_index("pts")
    grp = lax.axis_index("grp")
    core = me % 2
    half = (me // 2) % 2
    quad_z = (me // 4) % 8
    quad_y = me // 32
    base = me // 4 * 4
    other_core = base + half * 2 + (1 - core)
    other_chip = base + (1 - half) * 2 + core
    diagonal = base + (1 - half) * 2 + (1 - core)
    next_grp = (grp + 1) % 4
    last_grp = (grp + 3) % 4

    def place(dy, dz, chip_half):
        return (((quad_y + dy + 4) % 4) * 8 + (quad_z + dz + 8) % 8) * 4 + chip_half * 2 + core

    def copy_to(src, dst, ssem, rsem, pts=None, group=None):
        target = {"pts": pts} if group is None else {"grp": group}
        return pltpu.make_async_remote_copy(
            src_ref=src,
            dst_ref=dst,
            send_sem=ssem,
            recv_sem=rsem,
            device_id=target,
            device_id_type=MESH,
        )

    barrier = pltpu.get_barrier_semaphore()

    def greet(target):
        pl.semaphore_signal(barrier, inc=1, device_id=target, device_id_type=MESH)

    for dy in range(4):
        for dz in range(1, 4):
            greet({"pts": place(dy, dz, 0)})
            greet({"pts": place(dy, 8 - dz, 1)})
            greet({"pts": place(dy, (8 - dz) * (1 - half) + dz * half, half)})
        greet({"pts": place(dy, 4, 1 - half)})
        if dy:
            greet({"pts": place(dy, 0, half)})
    greet({"pts": other_core})
    greet({"pts": other_chip})
    greet({"pts": diagonal})
    greet({"grp": next_grp})
    greet({"grp": last_grp})

    slot = slot_ref[...]
    owner = slot // PATCH
    position = slot % PATCH
    index = jnp.where(owner // 128 == grp, owner % 128, 0)
    quad = index // 4
    dy_of = (quad // 8 - quad_y + 4) % 4
    dz_of = (quad % 8 - quad_z + 8) % 8
    turn = dz_of - 4
    place_of = 2 * jnp.abs(turn) - (turn < 0).astype(I32)
    block_of = place_of * 4 + dy_of
    inner = jnp.where(place_of % 2 == 1, place_of + half, place_of - 1 + half)
    kord_of = jnp.where(place_of == 0, 0, jnp.where(place_of == 7, 7, inner))
    in_block = onehot(iota((32, ROWS), 0) == block_of)
    upto = onehot(iota((ROWS, ROWS), 0) <= iota((ROWS, ROWS), 1))
    counted = mm(in_block, upto)
    rank = jnp.sum(in_block.astype(F32) * counted, axis=0, keepdims=True).astype(I32) - 1
    row_of = block_of * 16 + rank
    perm = onehot(iota((ROWS, ROWS), 0) == row_of)
    rows_sorted = mm(perm, x_ref[0]).astype(BF)
    xp[...] = rows_sorted
    code = (index % 4) * PATCH + position
    high = in_block * (code // 64).astype(BF)
    low = in_block * (code % 64).astype(BF)
    lane_of = (kord_of % 2 * 4 + dy_of) * 16 + rank
    spread = onehot(iota((128, ROWS), 0) == lane_of)
    tags = mm_nt(high, spread) * 64.0 + mm_nt(low, spread)
    for block in range(32):
        tag_send[block] = tags[block : block + 1]

    def columns_of(rows):
        padded = jnp.concatenate(
            [rows.astype(F32), jnp.zeros((128 - rows.shape[0], 128), F32)], axis=0
        )
        return jnp.transpose(padded).astype(I32)

    row_cols = columns_of(
        jnp.concatenate([row_of[:, t * 128 : t * 128 + 128] for t in range(4)], axis=0)
    )
    for t in range(4):
        home_m[t * 128 : t * 128 + 128] = onehot(iota((128, ROWS), 1) == row_cols[:, t : t + 1])

    vobuf[:, :, 128:] = jnp.ones((2, PATCH, 128), BF)
    normed = layer_norm(rows_sorted, gain_ref[0, 0:1], shift_ref[0, 0:1])
    projected = mm(normed, qkv_ref[0]).astype(BF)
    qbuf[...] = projected[:, :WIDTH]
    kbuf[:ROWS] = projected[:, WIDTH : 2 * WIDTH]
    vobuf[0, :ROWS, :128] = projected[:, 2 * WIDTH : 2 * WIDTH + 128]
    vobuf[1, :ROWS, :128] = projected[:, 2 * WIDTH + 128 :]

    pl.semaphore_wait(barrier, PEERS)
    pair = copy_to(x_ref.at[0], px, pair_sem.at[0], pair_sem.at[1], pts=other_core)
    pair.start()

    def tag_copy(block, s, pts):
        return copy_to(tag_send.at[block], tag_recv.at[s], tag_ssem, tag_rsem, pts=pts)

    def legs(turn_index):
        first = (3 - turn_index) // 3
        last = turn_index // 3
        even = (4 + turn_index, 1 - half * first, (2 * turn_index - 1 + half) * (1 - first))
        odd = (3 - turn_index, half * last, 2 * turn_index + 1 + half * (1 - last))
        return even, odd

    for part in range(4):
        for parity, (dz, chip_half, kord) in enumerate(legs(part)):
            for dy in range(4):
                block = (2 * part + parity) * 4 + dy
                if block == 28:
                    tag_recv[28] = tag_send[28]
                else:
                    tag_copy(block, kord * 4 + dy, place(dy, dz, chip_half)).start()

    pair.wait()
    normed = layer_norm(px[...], gain_ref[0, 0:1], shift_ref[0, 0:1])
    projected = mm(normed, qkv_ref[0, :, WIDTH:]).astype(BF)
    kbuf[ROWS:] = projected[:, :WIDTH]
    vobuf[0, ROWS:, :128] = projected[:, WIDTH : WIDTH + 128]
    vobuf[1, ROWS:, :128] = projected[:, WIDTH + 128 :]

    def feed_forward(rows, block):
        normed_ff = layer_norm(rows, gain_ref[block, 1:2], shift_ref[block, 1:2])
        hidden = gelu(mm(normed_ff, up_ref[block]) + upb_ref[block : block + 1]).astype(BF)
        down = mm(hidden, down_ref[block]) + outb_ref[block, 1:2]
        return (rows.astype(F32) + down).astype(BF)

    head_lane = iota((128, 128), 1) // 16

    def part_one(part, carry):
        rows = pl.ds(pl.multiple_of(part * 128, 128), 128)
        totals = {}

        def score(step):
            group, pair_index = step
            queries = qbuf[rows, group * 128 : group * 128 + 128]
            masked = [
                jnp.where(head_lane == head, queries, jnp.zeros_like(queries))
                for head in (2 * pair_index, 2 * pair_index + 1)
            ]
            return mm_nt(
                jnp.concatenate(masked, axis=0), kbuf[:, group * 128 : group * 128 + 128]
            )

        def finish(step, scores):
            group, pair_index = step
            weights = jnp.exp2(scores * SCALE).astype(BF)
            result = mm(weights, vobuf[group])
            for side in range(2):
                mine = result[side * 128 : side * 128 + 128]
                head = 2 * pair_index + side
                if head == 0:
                    totals[group] = (mine[:, :128], mine[:, 128:])
                else:
                    top, bottom = totals[group]
                    totals[group] = (
                        jnp.where(head_lane == head, mine[:, :128], top),
                        jnp.where(head_lane == head, mine[:, 128:], bottom),
                    )

        pipelined([(g, h) for g in range(2) for h in range(4)], score, finish)
        attended = jnp.concatenate(
            [(totals[g][0] / totals[g][1]).astype(BF) for g in range(2)], axis=1
        )
        mixed = xp[rows, :].astype(F32) + (mm(attended, proj_ref[0]) + outb_ref[0, 0:1])
        send_a[rows, :] = feed_forward(mixed.astype(BF), 0)
        for parity, (dz, chip_half, kord) in enumerate(legs(part)):
            for dy in range(4):
                block = (2 * part + parity) * 4 + dy

                def start(block=block, dz=dz, chip_half=chip_half, kord=kord, dy=dy):
                    copy_to(
                        send_a.at[pl.ds(block * 16, 16)],
                        recv_a.at[pl.ds((kord * 4 + dy) * 16, 16)],
                        ab_send,
                        ab_recv.at[kord],
                        pts=place(dy, dz, chip_half),
                    ).start()

                if parity == 1 and dy == 0:
                    pl.when(part < 3)(start)
                else:
                    start()
        return carry

    lax.fori_loop(0, 4, part_one, 0)
    recv_a[448:464] = send_a[448:464]

    def wait_bytes(view, sem):
        pltpu.make_async_copy(view, view, sem).wait()

    wait_bytes(tag_recv.at[pl.ds(0, 31)], tag_rsem)
    groups = []
    for t in range(4):
        total = tag_recv[8 * t]
        for s in range(1, 8):
            total = total + tag_recv[8 * t + s]
        groups.append(total)
    tag_quad[0] = jnp.concatenate(groups + [jnp.zeros((4, 128), F32)], axis=0)
    quad_copies = [
        copy_to(
            tag_quad.at[0], tag_quad.at[rel], quad_ssem.at[rel], quad_rsem.at[rel], pts=target
        )
        for rel, target in ((1, other_chip), (2, other_core), (3, diagonal))
    ]
    for one in quad_copies:
        one.start()

    low_lane = iota((128, 128), 1) < 64
    columns = pl.multiple_of(half * 128, 128)
    mine_first = core == 0

    def project_two(rows):
        normed_two = layer_norm(rows, gain_ref[1, 0:1], shift_ref[1, 0:1])
        parts = [
            mm(normed_two, qkv_ref[1, :, pl.ds(t * WIDTH + columns, 128)]) for t in range(3)
        ]
        turned = [pltpu.roll(part, 64, 1) for part in parts]
        low = [jnp.where(mine_first, parts[t], turned[t]) for t in range(3)]
        upper = [jnp.where(mine_first, turned[t], parts[t]) for t in range(3)]
        ones = jnp.ones((128, 128), F32)
        own = [jnp.where(low_lane, low[0], upper[1]), jnp.where(low_lane, low[2], ones)]
        other = [jnp.where(low_lane, upper[0], low[1]), jnp.where(low_lane, upper[2], ones)]
        return (
            jnp.concatenate(own, axis=1).astype(BF),
            jnp.concatenate(other, axis=1).astype(BF),
        )

    def z_copy(part):
        rows = pl.ds(part * 128, 128)
        return copy_to(
            recv_a.at[rows], zrows.at[rows], z_ssem.at[part], z_rsem.at[part], pts=other_chip
        )

    def d_copy(which, part):
        rows = pl.ds(part * 128, 128)
        sem = which * 4 + part
        return copy_to(
            dsend.at[which, rows],
            gath.at[2 + which, rows],
            d_ssem.at[sem],
            d_rsem.at[sem],
            pts=other_core,
        )

    for part in range(4):
        for kord in (2 * part, 2 * part + 1):
            count = 48 if kord == 7 else 64
            wait_bytes(recv_a.at[pl.ds(kord * 64, count)], ab_recv.at[kord])
        z_copy(part).start()
    for part in range(4):
        rows = slice(part * 128, part * 128 + 128)
        gath[0, rows], dsend[0, rows] = project_two(recv_a[rows])
        d_copy(0, part).start()

    for one in quad_copies:
        one.wait_recv()
    codes = jnp.concatenate([tag_quad[rel, 0:4] for rel in range(4)], axis=0).astype(I32)
    place_in = codes // PATCH
    counts = []
    for who in range(4):
        mine = (place_in == who).astype(F32)
        mine = jnp.sum(mine, axis=1, keepdims=True)
        counts.append(jnp.sum(mine, axis=0, keepdims=True).astype(I32))
    full = [count == PATCH for count in counts]
    start_at = jnp.zeros((1, 1), I32) + PATCH
    sorted_at = codes % PATCH
    firsts = []
    for who in range(4):
        sorted_at = sorted_at + jnp.where(
            place_in == who, jnp.where(full[who], 0, start_at), 0
        )
        firsts.append(jnp.where(full[who], 0, start_at))
        start_at = start_at + jnp.where(full[who], 0, counts[who])
    zero_full = full[0]
    end_one = jnp.where(full[0], counts[1], counts[0])
    end_two = PATCH - jnp.where(full[3], counts[2], counts[3])
    cols = columns_of(sorted_at)

    for t in range(16):
        lane_row = sorted_at[t : t + 1]

        def sort_block(block, carry, t=t, lane_row=lane_row):
            rows = pl.ds(pl.multiple_of(block * 256, 256), 256)
            sort_m[rows, t * 128 : t * 128 + 128] = onehot(
                iota((256, 128), 0) + block * 256 == lane_row
            )
            return carry

        lax.fori_loop(0, 8, sort_block, 0)
        unsort_m[t * 128 : t * 128 + 128] = onehot(iota((128, 2048), 1) == cols[:, t : t + 1])

    for part in range(4):
        rows = slice(part * 128, part * 128 + 128)
        z_copy(part).wait_recv()
        gath[1, rows], dsend[1, rows] = project_two(zrows[rows])
        d_copy(1, part).start()
    for which in range(2):
        for part in range(4):
            d_copy(which, part).wait_recv()

    def sort_rows(block, carry):
        rows = pl.ds(pl.multiple_of(block * 256, 256), 256)
        total = mm(sort_m[rows, 0:512], gath[0])
        for rel in range(1, 4):
            total = total + mm(sort_m[rows, rel * 512 : rel * 512 + 512], gath[rel])
        gs[rows, :] = total.astype(BF)
        return carry

    sort_rows(0, 0)
    sort_rows(4, 0)
    cross_out[...] = jnp.where(zero_full, gs[0:CROSS], gs[PATCH : PATCH + CROSS])
    cross = copy_to(cross_out, cross_in, cross_sem.at[0], cross_sem.at[1], group=next_grp)
    cross.start()
    lax.fori_loop(1, 4, sort_rows, 0)
    lax.fori_loop(5, 8, sort_rows, 0)
    cross.wait()
    first_quad = me < 4
    in_full = jnp.logical_and(first_quad, zero_full)
    in_rest = jnp.logical_and(first_quad, jnp.logical_not(zero_full))
    gs[0:CROSS] = jnp.where(in_full, cross_in[...], gs[0:CROSS])
    gs[PATCH : PATCH + CROSS] = jnp.where(in_rest, cross_in[...], gs[PATCH : PATCH + CROSS])
    for t in range(8):
        rows = slice(t * 256, t * 256 + 256)
        kpack[rows] = pltpu.roll(gs[rows, 0:128].astype(F32), 64, 1).astype(BF)

    head_lane_two = iota((256, 128), 1) // 16

    def attend(query_rows, key_rows, mask):
        held = []

        def score(head):
            queries = gs[query_rows, 0:128]
            masked = jnp.where(head_lane_two == head, queries, jnp.zeros_like(queries))
            return mm_nt(masked, kpack[key_rows])

        def finish(head, scores):
            weights = jnp.exp2(scores * SCALE)
            if mask is not None:
                weights = jnp.where(mask, weights, 0.0)
            result = mm(weights.astype(BF), gs[key_rows, 128:256])
            if held:
                held[0] = jnp.where(head_lane_two % 4 == head, result, held[0])
            else:
                held.append(result)

        pipelined(list(range(4)), score, finish)
        total = held[0]
        attended = total / pltpu.roll(total, 64, 1)
        both = jnp.where(iota((256, 128), 1) < 64, attended, pltpu.roll(attended, 64, 1))
        att_s[query_rows] = both.astype(BF)

    def attend_full(block, carry):
        attend(pl.ds(pl.multiple_of(block * 256, 256), 256), slice(0, PATCH), None)
        return carry

    def attend_rest(block):
        low_key, high_key = ((0, 512), (0, 768), (256, 1024), (512, 1024))[block]
        size = high_key - low_key
        key_at = iota((1, size), 1) + low_key
        query_at = iota((256, 1), 0) + block * 256
        key_part = (key_at >= end_one).astype(I32) + (key_at >= end_two).astype(I32)
        query_part = (query_at >= end_one).astype(I32) + (query_at >= end_two).astype(I32)
        attend(
            slice(PATCH + block * 256, PATCH + block * 256 + 256),
            slice(PATCH + low_key, PATCH + high_key),
            query_part == key_part,
        )

    attend_full(0, 0)
    attend_rest(0)
    catt_out[...] = jnp.where(zero_full, att_s[0:CROSS], att_s[PATCH : PATCH + CROSS])
    cross_back = copy_to(catt_out, catt_in, catt_sem.at[0], catt_sem.at[1], group=last_grp)
    cross_back.start()
    lax.fori_loop(1, 4, attend_full, 0)
    for block in range(1, 4):
        attend_rest(block)
    cross_back.wait()
    att_s[0:CROSS] = jnp.where(in_full, catt_in[...], att_s[0:CROSS])
    att_s[PATCH : PATCH + CROSS] = jnp.where(
        in_rest, catt_in[...], att_s[PATCH : PATCH + CROSS]
    )

    low_lane_two = iota((256, 128), 1) < 64

    def unsorted(rel, part):
        at = rel * 512 + part * 256
        return mm(unsort_m[at : at + 256], att_s[...])

    def za_copy(part):
        rows = pl.ds(part * 256, 256)
        return copy_to(
            zatt_out.at[rows], zatt_in.at[rows], za_ssem.at[part], za_rsem.at[part], pts=other_chip
        )

    def da_copy(part):
        rows = pl.ds(part * 256, 256)
        return copy_to(
            datt_out.at[rows], datt_in.at[rows], da_ssem.at[part], da_rsem.at[part], pts=other_core
        )

    for part in range(2):
        rows = slice(part * 256, part * 256 + 256)
        zatt_out[rows] = jnp.where(low_lane_two, unsorted(1, part), unsorted(3, part)).astype(BF)
        za_copy(part).start()
    for part in range(2):
        rows = slice(part * 256, part * 256 + 256)
        for_other = unsorted(2, part)
        za_copy(part).wait_recv()
        arrived = zatt_in[rows].astype(F32)
        datt_out[rows] = jnp.where(low_lane_two, for_other, arrived).astype(BF)
        da_copy(part).start()
        own_att[rows] = jnp.where(
            low_lane_two, unsorted(0, part), pltpu.roll(arrived, 64, 1)
        ).astype(BF)

    def proj_rows(chip_half, chip_core):
        at = pl.multiple_of((chip_half * 2 + chip_core) * 64, 64)
        return proj_ref[1, pl.ds(at, 64), :]

    weights_a = jnp.concatenate([proj_rows(half, core), proj_rows(1 - half, core)], axis=0)
    weights_b = jnp.concatenate([proj_rows(half, 1 - core), proj_rows(1 - half, 1 - core)], axis=0)
    for part in range(2):
        da_copy(part).wait_recv()

    def part_two(part, carry):
        rows = pl.ds(pl.multiple_of(part * 128, 128), 128)
        out_rows = mm(own_att[rows, :], weights_a) + mm(datt_in[rows, :], weights_b)
        mixed = recv_a[rows, :].astype(F32) + (out_rows + outb_ref[1, 0:1])
        ret_send[rows, :] = feed_forward(mixed.astype(BF), 1)
        first = (3 - part) // 3
        last = part // 3
        even = (4 - part + half * (2 * part), 1 - half * first, (2 * part - 1 + half) * (1 - first))
        odd = (
            3 - part + half * (2 + 2 * part),
            half * last,
            2 * part + 1 + half * (1 - last),
        )
        for parity, (dz, chip_half, place_at) in enumerate((even, odd)):
            for dy in range(4):
                s = (2 * part + parity) * 4 + dy

                def start(s=s, dz=dz, chip_half=chip_half, place_at=place_at, dy=dy):
                    copy_to(
                        ret_send.at[pl.ds(s * 16, 16)],
                        home.at[pl.ds((place_at * 4 + dy) * 16, 16)],
                        rt_ssem,
                        rt_rsem.at[place_at],
                        pts=place(-dy, -dz, chip_half),
                    ).start()

                if parity == 1 and dy == 0:
                    pl.when(part < 3)(start)
                else:
                    start()
        return carry

    lax.fori_loop(0, 4, part_two, 0)
    home[448:464] = ret_send[448:464]
    for place_at in range(8):
        count = 48 if place_at == 7 else 64
        wait_bytes(home.at[pl.ds(place_at * 64, count)], rt_rsem.at[place_at])
    out_ref[0] = mm(home_m[...], home[...]).astype(BF)

    wait_bytes(tag_send.at[pl.ds(0, 31)], tag_ssem)
    for one in quad_copies:
        one.wait_send()
    wait_bytes(send_a.at[pl.ds(0, 496)], ab_send)
    for part in range(4):
        z_copy(part).wait_send()
    for which in range(2):
        for part in range(4):
            d_copy(which, part).wait_send()
    for part in range(2):
        za_copy(part).wait_send()
        da_copy(part).wait_send()
    wait_bytes(ret_send.at[pl.ds(0, 496)], rt_ssem)


def on_device(
    features,
    hilbert_slot,
    hilbert_count,
    norm_gain,
    norm_shift,
    qkv_weight,
    proj_weight,
    up_weight,
    up_bias,
    down_weight,
    out_bias,
):
    vmem = pl.BlockSpec(memory_space=pltpu.VMEM)
    sems = pltpu.SemaphoreType.DMA
    rows_buffer = pltpu.VMEM((ROWS, WIDTH), BF)
    half_buffer = pltpu.VMEM((ROWS, 128), BF)
    scratch = [
        rows_buffer,
        rows_buffer,
        rows_buffer,
        pltpu.VMEM((PATCH, WIDTH), BF),
        pltpu.VMEM((2, PATCH, WIDTH), BF),
        rows_buffer,
        rows_buffer,
        pltpu.VMEM((32, 1, 128), F32),
        pltpu.VMEM((32, 1, 128), F32),
        pltpu.VMEM((4, 8, 128), F32),
        rows_buffer,
        pltpu.VMEM((4, ROWS, WIDTH), BF),
        pltpu.VMEM((2, ROWS, WIDTH), BF),
        pltpu.VMEM((2 * PATCH, 2 * PATCH), BF),
        pltpu.VMEM((2 * PATCH, 2 * PATCH), BF),
        pltpu.VMEM((ROWS, ROWS), BF),
        pltpu.VMEM((2 * PATCH, WIDTH), BF),
        pltpu.VMEM((2 * PATCH, 128), BF),
        pltpu.VMEM((CROSS, WIDTH), BF),
        pltpu.VMEM((CROSS, WIDTH), BF),
        pltpu.VMEM((2 * PATCH, 128), BF),
        pltpu.VMEM((CROSS, 128), BF),
        pltpu.VMEM((CROSS, 128), BF),
        half_buffer,
        half_buffer,
        half_buffer,
        half_buffer,
        half_buffer,
        rows_buffer,
        rows_buffer,
        sems,
        sems((8,)),
        sems,
        sems,
        sems((4,)),
        sems((4,)),
        sems((2,)),
        sems((4,)),
        sems((4,)),
        sems((8,)),
        sems((8,)),
        sems((2,)),
        sems((2,)),
        sems((2,)),
        sems((2,)),
        sems((2,)),
        sems((2,)),
        sems,
        sems((8,)),
    ]
    return pl.pallas_call(
        kernel,
        out_shape=jax.ShapeDtypeStruct((1, ROWS, WIDTH), BF),
        in_specs=[vmem] * 10,
        out_specs=vmem,
        scratch_shapes=scratch,
        compiler_params=pltpu.CompilerParams(
            collective_id=0, has_side_effects=True, vmem_limit_bytes=60 * 2**20
        ),
    )(
        features,
        hilbert_slot,
        norm_gain,
        norm_shift,
        qkv_weight,
        proj_weight,
        up_weight,
        up_bias,
        down_weight,
        out_bias,
    )


def solution(mesh):
    return jax.shard_map(
        on_device,
        mesh=mesh,
        in_specs=(
            P("grp", "pts", None),
            P("grp", "pts"),
            P("grp", "pts"),
            P(),
            P(),
            P(),
            P(),
            P(),
            P(),
            P(),
            P(),
        ),
        out_specs=P("grp", "pts", None),
        check_vma=False,
    )
```

time: 376 us -> 89.6 us (0.24); the launches traced: 370 us -> 89.5 us
  local copies, waits for them, and re-layouts: 118 us -> 1.67 us
  Pallas kernels: 0 us -> 87.8 us
  matrix products: 73.1 us -> 0 us
  blocking collectives: 64 us -> 0 us
  waiting for transfers between devices: 54.4 us -> 0 us
  starting transfers between devices: 46.1 us -> 0 us
  other arithmetic: 13.2 us -> 0 us
    scatter x4 -> x0, local copies, waits for them, and re-layouts: 98.6 us -> none  [the longest x1 55.5 us: on_device(): send_rows = jnp.zeros((owner_count, pair_slots, feature_width), jnp.bfloa...]
    pallas_call x0 -> x1, Pallas kernels: none -> 87.8 us  [on_device(): pl.pallas_call(kernel, out_shape=jax.ShapeDtypeStruct((1, ROWS, WIDTH), B...]
    dot_general x70 -> x0, matrix products: 73.1 us -> none  [the longest x32 27.3 us: one_head(): jnp.einsum('dk,qk->dq', v_one, weights_low, preferred_element_type=jnp.fl...]
    all_to_all x1 -> x0, blocking collectives: 64 us -> none  [on_device(): lax.all_to_all(reply_rows, 'pts', split_axis=0, concat_axis=0, tiled=True)]
    all_to_all x2 -> x0, waiting for transfers between devices: 52.8 us -> none  [the longest x1 52.8 us: on_device(): lax.all_to_all(send_rows, 'pts', split_axis=0, concat_axis=0, tiled=True)]
    all_to_all x2 -> x0, starting transfers between devices: 30.9 us -> none  [the longest x1 16.5 us: on_device(): lax.all_to_all(send_rows, 'pts', split_axis=0, concat_axis=0, tiled=True)]
    ppermute x3 -> x0, starting transfers between devices: 15.3 us -> none  [the longest x1 8.79 us: swapped(): lax.ppermute(shard, axis, [(i, i ^ 1 << distance) for i in range(lax.axis...]
    gather x2 -> x0, local copies, waits for them, and re-layouts: 13.1 us -> none  [the longest x1 7.5 us: on_device(): reply_table[local_tags].reshape(owner_count, pair_slots, feature_width)]
  transfers between devices with their start and end apart: 5 -> 0, of which waited for: 2 -> 0; matrix products, arithmetic and copies ran while one was open for 31% -> 0% of each run, Pallas kernels for 0% -> 0%
where the time goes in v1:
time: 89.6 us; the launch traced here: 89.5 us
  Pallas kernels  87.8 us (98%)
  local copies, waits for them, and re-layouts  1.67 us (2%)
    pallas_call x1, Pallas kernels, on_device(): pl.pallas_call(kernel, out_shape=jax.ShapeDtypeStruct((1, ROWS, WIDTH), B...  87.8 us

profile of v1, /device:TPU:1, one launch (start us, length us, event | category | flops | bytes accessed | tf_op | source)
XLA Modules:
  0.0 89.5 jit_solution(3725133609305665239)
XLA Ops:
  0.0 87.8 %shard_map.100 = bf16[1,512,256]{2,1,0:T(8,128)(2,1)} custom-call(bf16[1,512,256]{2,1,0:T(8,128)(2,1)} %x_ref.1, s32[1,512]{1,0:T(1,128)} %slot_ref.1, f32[2,2,256]{2,1,0:T(2,128)} %gain_ref.1, f32[2,2,256]{2,1,0:T(2,128)} %shift_ref.1, bf16[2,256,768]{2,1,0:T(8,128)(2,1)} %qkv_ref.1, bf16[2,256,256]{2,1,0:T(8,128)(2,1)} %proj_ref.1, ...), custom_call_target="tpu_custom_call" | custom-call | tf_op jit(solution)/shard_map/pallas_call | solution.py:671
  87.8 1.7 %copy.12 = bf16[1,512,256]{2,1,0:T(8,128)(2,1)} copy(bf16[1,512,256]{2,1,0:T(8,128)(2,1)} %shard_map.100) | data formatting | bytes 524288

commit v2 on v1

--- a/solution.py
+++ b/solution.py
@@ -60,15 +60,21 @@
     slot_ref,
     gain_ref,
     shift_ref,
+    qkv_any,
+    proj_any,
+    up_any,
+    upb_ref,
+    down_any,
+    outb_ref,
+    out_ref,
     qkv_ref,
     proj_ref,
     up_ref,
-    upb_ref,
     down_ref,
-    outb_ref,
-    out_ref,
+    weight_sem,
     px,
     xp,
+    acc,
     qbuf,
     kbuf,
     vobuf,
@@ -83,6 +89,7 @@
     sort_m,
     unsort_m,
     home_m,
+    gacc,
     gs,
     kpack,
     cross_out,
@@ -93,6 +100,7 @@
     zatt_out,
     zatt_in,
     own_att,
+    other_att,
     datt_out,
     datt_in,
     ret_send,
@@ -144,6 +152,9 @@
             device_id_type=MESH,
         )
 
+    def wait_bytes(view, sem):
+        pltpu.make_async_copy(view, view, sem).wait()
+
     barrier = pltpu.get_barrier_semaphore()
 
     def greet(target):
@@ -162,6 +173,20 @@
     greet({"pts": diagonal})
     greet({"grp": next_grp})
     greet({"grp": last_grp})
+
+    loads = [
+        pltpu.make_async_copy(source, target, weight_sem.at[index])
+        for index, (source, target) in enumerate(
+            (
+                (qkv_any, qkv_ref),
+                (proj_any, proj_ref),
+                (up_any, up_ref),
+                (down_any, down_ref),
+            )
+        )
+    ]
+    for one in loads:
+        one.start()
 
     slot = slot_ref[...]
     owner = slot // PATCH
@@ -198,13 +223,8 @@
         )
         return jnp.transpose(padded).astype(I32)
 
-    row_cols = columns_of(
-        jnp.concatenate([row_of[:, t * 128 : t * 128 + 128] for t in range(4)], axis=0)
-    )
-    for t in range(4):
-        home_m[t * 128 : t * 128 + 128] = onehot(iota((128, ROWS), 1) == row_cols[:, t : t + 1])
-
     vobuf[:, :, 128:] = jnp.ones((2, PATCH, 128), BF)
+    loads[0].wait()
     normed = layer_norm(rows_sorted, gain_ref[0, 0:1], shift_ref[0, 0:1])
     projected = mm(normed, qkv_ref[0]).astype(BF)
     qbuf[...] = projected[:, :WIDTH]
@@ -212,36 +232,6 @@
     vobuf[0, :ROWS, :128] = projected[:, 2 * WIDTH : 2 * WIDTH + 128]
     vobuf[1, :ROWS, :128] = projected[:, 2 * WIDTH + 128 :]
 
-    pl.semaphore_wait(barrier, PEERS)
-    pair = copy_to(x_ref.at[0], px, pair_sem.at[0], pair_sem.at[1], pts=other_core)
-    pair.start()
-
-    def tag_copy(block, s, pts):
-        return copy_to(tag_send.at[block], tag_recv.at[s], tag_ssem, tag_rsem, pts=pts)
-
-    def legs(turn_index):
-        first = (3 - turn_index) // 3
-        last = turn_index // 3
-        even = (4 + turn_index, 1 - half * first, (2 * turn_index - 1 + half) * (1 - first))
-        odd = (3 - turn_index, half * last, 2 * turn_index + 1 + half * (1 - last))
-        return even, odd
-
-    for part in range(4):
-        for parity, (dz, chip_half, kord) in enumerate(legs(part)):
-            for dy in range(4):
-                block = (2 * part + parity) * 4 + dy
-                if block == 28:
-                    tag_recv[28] = tag_send[28]
-                else:
-                    tag_copy(block, kord * 4 + dy, place(dy, dz, chip_half)).start()
-
-    pair.wait()
-    normed = layer_norm(px[...], gain_ref[0, 0:1], shift_ref[0, 0:1])
-    projected = mm(normed, qkv_ref[0, :, WIDTH:]).astype(BF)
-    kbuf[ROWS:] = projected[:, :WIDTH]
-    vobuf[0, ROWS:, :128] = projected[:, WIDTH : WIDTH + 128]
-    vobuf[1, ROWS:, :128] = projected[:, WIDTH + 128 :]
-
     def feed_forward(rows, block):
         normed_ff = layer_norm(rows, gain_ref[block, 1:2], shift_ref[block, 1:2])
         hidden = gelu(mm(normed_ff, up_ref[block]) + upb_ref[block : block + 1]).astype(BF)
@@ -250,8 +240,7 @@
 
     head_lane = iota((128, 128), 1) // 16
 
-    def part_one(part, carry):
-        rows = pl.ds(pl.multiple_of(part * 128, 128), 128)
+    def attend_one(rows, keys):
         totals = {}
 
         def score(step):
@@ -262,13 +251,13 @@
                 for head in (2 * pair_index, 2 * pair_index + 1)
             ]
             return mm_nt(
-                jnp.concatenate(masked, axis=0), kbuf[:, group * 128 : group * 128 + 128]
+                jnp.concatenate(masked, axis=0), kbuf[keys, group * 128 : group * 128 + 128]
             )
 
         def finish(step, scores):
             group, pair_index = step
             weights = jnp.exp2(scores * SCALE).astype(BF)
-            result = mm(weights, vobuf[group])
+            result = mm(weights, vobuf[group, keys])
             for side in range(2):
                 mine = result[side * 128 : side * 128 + 128]
                 head = 2 * pair_index + side
@@ -282,8 +271,77 @@
                     )
 
         pipelined([(g, h) for g in range(2) for h in range(4)], score, finish)
+        return totals
+
+    def own_keys(part, carry):
+        rows = pl.ds(pl.multiple_of(part * 128, 128), 128)
+        totals = attend_one(rows, slice(0, ROWS))
+        for group in range(2):
+            acc[rows, group * 256 : group * 256 + 128] = totals[group][0]
+            acc[rows, group * 256 + 128 : group * 256 + 256] = totals[group][1]
+        return carry
+
+    lax.fori_loop(0, 3, own_keys, 0)
+    pl.semaphore_wait(barrier, PEERS)
+    pair = copy_to(x_ref.at[0], px, pair_sem.at[0], pair_sem.at[1], pts=other_core)
+    pair.start()
+
+    def tag_copy(block, s, pts):
+        return copy_to(tag_send.at[block], tag_recv.at[s], tag_ssem, tag_rsem, pts=pts)
+
+    def legs(turn_index):
+        first = (3 - turn_index) // 3
+        last = turn_index // 3
+        even = (4 + turn_index, 1 - half * first, (2 * turn_index - 1 + half) * (1 - first))
+        odd = (3 - turn_index, half * last, 2 * turn_index + 1 + half * (1 - last))
+        return even, odd
+
+    for part in range(4):
+        for parity, (dz, chip_half, kord) in enumerate(legs(part)):
+            for dy in range(4):
+                block = (2 * part + parity) * 4 + dy
+                if block == 28:
+                    tag_recv[28] = tag_send[28]
+                else:
+                    tag_copy(block, kord * 4 + dy, place(dy, dz, chip_half)).start()
+
+    lax.fori_loop(3, 4, own_keys, 0)
+    for one in loads[1:]:
+        one.wait()
+    pair.wait()
+    normed = layer_norm(px[...], gain_ref[0, 0:1], shift_ref[0, 0:1])
+    projected = mm(normed, qkv_ref[0, :, WIDTH:]).astype(BF)
+    kbuf[ROWS:] = projected[:, :WIDTH]
+    vobuf[0, ROWS:, :128] = projected[:, WIDTH : WIDTH + 128]
+    vobuf[1, ROWS:, :128] = projected[:, WIDTH + 128 :]
+
+
+    quad_copies = [
+        copy_to(
+            tag_quad.at[0], tag_quad.at[rel], quad_ssem.at[rel], quad_rsem.at[rel], pts=target
+        )
+        for rel, target in ((1, other_chip), (2, other_core), (3, diagonal))
+    ]
+
+    def share_tags():
+        wait_bytes(tag_recv.at[pl.ds(0, 31)], tag_rsem)
+        groups = []
+        for t in range(4):
+            total = tag_recv[8 * t]
+            for s in range(1, 8):
+                total = total + tag_recv[8 * t + s]
+            groups.append(total)
+        tag_quad[0] = jnp.concatenate(groups + [jnp.zeros((4, 128), F32)], axis=0)
+        for one in quad_copies:
+            one.start()
+
+    def part_one(part, carry):
+        rows = pl.ds(pl.multiple_of(part * 128, 128), 128)
+        totals = attend_one(rows, slice(ROWS, PATCH))
+        tops = [acc[rows, g * 256 : g * 256 + 128] + totals[g][0] for g in range(2)]
+        bottoms = [acc[rows, g * 256 + 128 : g * 256 + 256] + totals[g][1] for g in range(2)]
         attended = jnp.concatenate(
-            [(totals[g][0] / totals[g][1]).astype(BF) for g in range(2)], axis=1
+            [(tops[g] / bottoms[g]).astype(BF) for g in range(2)], axis=1
         )
         mixed = xp[rows, :].astype(F32) + (mm(attended, proj_ref[0]) + outb_ref[0, 0:1])
         send_a[rows, :] = feed_forward(mixed.astype(BF), 0)
@@ -304,30 +362,11 @@
                     pl.when(part < 3)(start)
                 else:
                     start()
+        pl.when(part == 1)(share_tags)
         return carry
 
     lax.fori_loop(0, 4, part_one, 0)
     recv_a[448:464] = send_a[448:464]
-
-    def wait_bytes(view, sem):
-        pltpu.make_async_copy(view, view, sem).wait()
-
-    wait_bytes(tag_recv.at[pl.ds(0, 31)], tag_rsem)
-    groups = []
-    for t in range(4):
-        total = tag_recv[8 * t]
-        for s in range(1, 8):
-            total = total + tag_recv[8 * t + s]
-        groups.append(total)
-    tag_quad[0] = jnp.concatenate(groups + [jnp.zeros((4, 128), F32)], axis=0)
-    quad_copies = [
-        copy_to(
-            tag_quad.at[0], tag_quad.at[rel], quad_ssem.at[rel], quad_rsem.at[rel], pts=target
-        )
-        for rel, target in ((1, other_chip), (2, other_core), (3, diagonal))
-    ]
-    for one in quad_copies:
-        one.start()
 
     low_lane = iota((128, 128), 1) < 64
     columns = pl.multiple_of(half * 128, 128)
@@ -365,16 +404,6 @@
             d_rsem.at[sem],
             pts=other_core,
         )
-
-    for part in range(4):
-        for kord in (2 * part, 2 * part + 1):
-            count = 48 if kord == 7 else 64
-            wait_bytes(recv_a.at[pl.ds(kord * 64, count)], ab_recv.at[kord])
-        z_copy(part).start()
-    for part in range(4):
-        rows = slice(part * 128, part * 128 + 128)
-        gath[0, rows], dsend[0, rows] = project_two(recv_a[rows])
-        d_copy(0, part).start()
 
     for one in quad_copies:
         one.wait_recv()
@@ -400,10 +429,10 @@
     end_two = PATCH - jnp.where(full[3], counts[2], counts[3])
     cols = columns_of(sorted_at)
 
-    for t in range(16):
+    def build_onehots(t):
         lane_row = sorted_at[t : t + 1]
 
-        def sort_block(block, carry, t=t, lane_row=lane_row):
+        def sort_block(block, carry):
             rows = pl.ds(pl.multiple_of(block * 256, 256), 256)
             sort_m[rows, t * 128 : t * 128 + 128] = onehot(
                 iota((256, 128), 0) + block * 256 == lane_row
@@ -414,20 +443,48 @@
         unsort_m[t * 128 : t * 128 + 128] = onehot(iota((128, 2048), 1) == cols[:, t : t + 1])
 
     for part in range(4):
+        for t in range(4 * part, 4 * part + 4):
+            build_onehots(t)
+        for kord in (2 * part, 2 * part + 1):
+            count = 48 if kord == 7 else 64
+            wait_bytes(recv_a.at[pl.ds(kord * 64, count)], ab_recv.at[kord])
+        z_copy(part).start()
+        rows = slice(part * 128, part * 128 + 128)
+        gath[0, rows], dsend[0, rows] = project_two(recv_a[rows])
+        d_copy(0, part).start()
+
+    def partner_rows(part):
         rows = slice(part * 128, part * 128 + 128)
         z_copy(part).wait_recv()
         gath[1, rows], dsend[1, rows] = project_two(zrows[rows])
         d_copy(1, part).start()
-    for which in range(2):
-        for part in range(4):
-            d_copy(which, part).wait_recv()
+
+    def sort_some(rows, rels):
+        total = mm(sort_m[rows, rels[0] * 512 : rels[0] * 512 + 512], gath[rels[0]])
+        for rel in rels[1:]:
+            total = total + mm(sort_m[rows, rel * 512 : rel * 512 + 512], gath[rel])
+        return total
+
+    def sort_own(block, carry):
+        rows = pl.ds(pl.multiple_of(block * 256, 256), 256)
+        gacc[rows, :] = sort_some(rows, (0, 2))
+        return carry
+
+    partner_rows(0)
+    partner_rows(1)
+    for part in range(4):
+        d_copy(0, part).wait_recv()
+    lax.fori_loop(0, 8, sort_own, 0)
+    partner_rows(2)
+    partner_rows(3)
+    for part in range(4):
+        d_copy(1, part).wait_recv()
 
     def sort_rows(block, carry):
         rows = pl.ds(pl.multiple_of(block * 256, 256), 256)
-        total = mm(sort_m[rows, 0:512], gath[0])
-        for rel in range(1, 4):
-            total = total + mm(sort_m[rows, rel * 512 : rel * 512 + 512], gath[rel])
+        total = gacc[rows, :] + sort_some(rows, (1, 3))
         gs[rows, :] = total.astype(BF)
+        kpack[rows, :] = pltpu.roll(total[:, 0:128], 64, 1).astype(BF)
         return carry
 
     sort_rows(0, 0)
@@ -443,8 +500,7 @@
     in_rest = jnp.logical_and(first_quad, jnp.logical_not(zero_full))
     gs[0:CROSS] = jnp.where(in_full, cross_in[...], gs[0:CROSS])
     gs[PATCH : PATCH + CROSS] = jnp.where(in_rest, cross_in[...], gs[PATCH : PATCH + CROSS])
-    for t in range(8):
-        rows = slice(t * 256, t * 256 + 256)
+    for rows in (slice(0, CROSS), slice(PATCH, PATCH + CROSS)):
         kpack[rows] = pltpu.roll(gs[rows, 0:128].astype(F32), 64, 1).astype(BF)
 
     head_lane_two = iota((256, 128), 1) // 16
@@ -504,38 +560,31 @@
         in_rest, catt_in[...], att_s[PATCH : PATCH + CROSS]
     )
 
-    low_lane_two = iota((256, 128), 1) < 64
-
-    def unsorted(rel, part):
-        at = rel * 512 + part * 256
-        return mm(unsort_m[at : at + 256], att_s[...])
+    def unsorted(rel, at, size):
+        return mm(unsort_m[rel * 512 + at : rel * 512 + at + size], att_s[...])
 
     def za_copy(part):
-        rows = pl.ds(part * 256, 256)
+        rows = pl.ds(part * 128, 128)
         return copy_to(
             zatt_out.at[rows], zatt_in.at[rows], za_ssem.at[part], za_rsem.at[part], pts=other_chip
         )
 
     def da_copy(part):
-        rows = pl.ds(part * 256, 256)
+        rows = pl.ds(part * 128, 128)
         return copy_to(
             datt_out.at[rows], datt_in.at[rows], da_ssem.at[part], da_rsem.at[part], pts=other_core
         )
 
+    low_lane_two = iota((256, 128), 1) < 64
     for part in range(2):
         rows = slice(part * 256, part * 256 + 256)
-        zatt_out[rows] = jnp.where(low_lane_two, unsorted(1, part), unsorted(3, part)).astype(BF)
-        za_copy(part).start()
-    for part in range(2):
-        rows = slice(part * 256, part * 256 + 256)
-        for_other = unsorted(2, part)
-        za_copy(part).wait_recv()
-        arrived = zatt_in[rows].astype(F32)
-        datt_out[rows] = jnp.where(low_lane_two, for_other, arrived).astype(BF)
-        da_copy(part).start()
-        own_att[rows] = jnp.where(
-            low_lane_two, unsorted(0, part), pltpu.roll(arrived, 64, 1)
+        zatt_out[rows] = jnp.where(
+            low_lane_two, unsorted(1, part * 256, 256), unsorted(3, part * 256, 256)
         ).astype(BF)
+        za_copy(2 * part).start()
+        za_copy(2 * part + 1).start()
+    other_att[...] = unsorted(2, 0, ROWS)
+    own_att[...] = unsorted(0, 0, ROWS).astype(BF)
 
     def proj_rows(chip_half, chip_core):
         at = pl.multiple_of((chip_half * 2 + chip_core) * 64, 64)
@@ -543,11 +592,20 @@
 
     weights_a = jnp.concatenate([proj_rows(half, core), proj_rows(1 - half, core)], axis=0)
     weights_b = jnp.concatenate([proj_rows(half, 1 - core), proj_rows(1 - half, 1 - core)], axis=0)
-    for part in range(2):
+
+    def regroup(part):
+        rows = pl.ds(pl.multiple_of(part * 128, 128), 128)
+        za_copy(part).wait_recv()
+        arrived = zatt_in[rows, :].astype(F32)
+        datt_out[rows, :] = jnp.where(low_lane, other_att[rows, :], arrived).astype(BF)
+        da_copy(part).start()
+        own_att[rows, :] = jnp.where(
+            low_lane, own_att[rows, :], pltpu.roll(arrived, 64, 1).astype(BF)
+        )
+
+    def part_two(part):
+        rows = pl.ds(pl.multiple_of(part * 128, 128), 128)
         da_copy(part).wait_recv()
-
-    def part_two(part, carry):
-        rows = pl.ds(pl.multiple_of(part * 128, 128), 128)
         out_rows = mm(own_att[rows, :], weights_a) + mm(datt_in[rows, :], weights_b)
         mixed = recv_a[rows, :].astype(F32) + (out_rows + outb_ref[1, 0:1])
         ret_send[rows, :] = feed_forward(mixed.astype(BF), 1)
@@ -576,9 +634,18 @@
                     pl.when(part < 3)(start)
                 else:
                     start()
+
+    def return_step(step, carry):
+        pl.when(step < 4)(lambda: regroup(step))
+        pl.when(step > 0)(lambda: part_two(step - 1))
         return carry
 
-    lax.fori_loop(0, 4, part_two, 0)
+    lax.fori_loop(0, 5, return_step, 0)
+    row_cols = columns_of(
+        jnp.concatenate([row_of[:, t * 128 : t * 128 + 128] for t in range(4)], axis=0)
+    )
+    for t in range(4):
+        home_m[t * 128 : t * 128 + 128] = onehot(iota((128, ROWS), 1) == row_cols[:, t : t + 1])
     home[448:464] = ret_send[448:464]
     for place_at in range(8):
         count = 48 if place_at == 7 else 64
@@ -594,7 +661,7 @@
     for which in range(2):
         for part in range(4):
             d_copy(which, part).wait_send()
-    for part in range(2):
+    for part in range(4):
         za_copy(part).wait_send()
         da_copy(part).wait_send()
     wait_bytes(ret_send.at[pl.ds(0, 496)], rt_ssem)
@@ -617,9 +684,16 @@
     sems = pltpu.SemaphoreType.DMA
     rows_buffer = pltpu.VMEM((ROWS, WIDTH), BF)
     half_buffer = pltpu.VMEM((ROWS, 128), BF)
+    any_space = pl.BlockSpec(memory_space=pl.ANY)
     scratch = [
+        pltpu.VMEM((2, WIDTH, 3 * WIDTH), BF),
+        pltpu.VMEM((2, WIDTH, WIDTH), BF),
+        pltpu.VMEM((2, WIDTH, 4 * WIDTH), BF),
+        pltpu.VMEM((2, 4 * WIDTH, WIDTH), BF),
+        sems((4,)),
         rows_buffer,
         rows_buffer,
+        pltpu.VMEM((ROWS, 2 * WIDTH), F32),
         rows_buffer,
         pltpu.VMEM((PATCH, WIDTH), BF),
         pltpu.VMEM((2, PATCH, WIDTH), BF),
@@ -634,6 +708,7 @@
         pltpu.VMEM((2 * PATCH, 2 * PATCH), BF),
         pltpu.VMEM((2 * PATCH, 2 * PATCH), BF),
         pltpu.VMEM((ROWS, ROWS), BF),
+        pltpu.VMEM((2 * PATCH, WIDTH), F32),
         pltpu.VMEM((2 * PATCH, WIDTH), BF),
         pltpu.VMEM((2 * PATCH, 128), BF),
         pltpu.VMEM((CROSS, WIDTH), BF),
@@ -644,6 +719,7 @@
         half_buffer,
         half_buffer,
         half_buffer,
+        pltpu.VMEM((ROWS, 128), F32),
         half_buffer,
         half_buffer,
         rows_buffer,
@@ -661,17 +737,17 @@
         sems((8,)),
         sems((2,)),
         sems((2,)),
-        sems((2,)),
-        sems((2,)),
-        sems((2,)),
-        sems((2,)),
+        sems((4,)),
+        sems((4,)),
+        sems((4,)),
+        sems((4,)),
         sems,
         sems((8,)),
     ]
     return pl.pallas_call(
         kernel,
         out_shape=jax.ShapeDtypeStruct((1, ROWS, WIDTH), BF),
-        in_specs=[vmem] * 10,
+        in_specs=[vmem] * 4 + [any_space] * 3 + [vmem, any_space, vmem],
         out_specs=vmem,
         scratch_shapes=scratch,
         compiler_params=pltpu.CompilerParams(

time: 89.6 us -> 86.8 us (0.969)
  Pallas kernels: 87.8 us -> 84.9 us
    pallas_call x1, Pallas kernels: 87.8 us -> 84.9 us  [on_device(): pl.pallas_call(kernel, out_shape=jax.ShapeDtypeStruct((1, ROWS, WIDTH), B...]
where the time goes in v2:
time: 86.8 us; the launch traced here: 86.6 us
  Pallas kernels  84.9 us (98%)
  local copies, waits for them, and re-layouts  1.67 us (2%)
    pallas_call x1, Pallas kernels, on_device(): pl.pallas_call(kernel, out_shape=jax.ShapeDtypeStruct((1, ROWS, WIDTH), B...  84.9 us

profile of v2, /device:TPU:1, one launch (start us, length us, event | category | flops | bytes accessed | tf_op | source)
XLA Modules:
  0.0 86.6 jit_solution(14239526032479228915)
XLA Ops:
  0.0 84.9 %shard_map.100 = bf16[1,512,256]{2,1,0:T(8,128)(2,1)} custom-call(bf16[1,512,256]{2,1,0:T(8,128)(2,1)} %x_ref.1, s32[1,512]{1,0:T(1,128)} %slot_ref.1, f32[2,2,256]{2,1,0:T(2,128)} %gain_ref.1, f32[2,2,256]{2,1,0:T(2,128)} %shift_ref.1, bf16[2,256,768]{2,1,0:T(8,128)(2,1)} %qkv_any.1, bf16[2,256,256]{2,1,0:T(8,128)(2,1)} %proj_any.1, ...), custom_call_target="tpu_custom_call" | custom-call | tf_op jit(solution)/shard_map/pallas_call | solution.py:747
  84.9 1.7 %copy.12 = bf16[1,512,256]{2,1,0:T(8,128)(2,1)} copy(bf16[1,512,256]{2,1,0:T(8,128)(2,1)} %shard_map.100) | data formatting | bytes 524288

commit v3 on v2

--- a/solution.py
+++ b/solution.py
@@ -12,7 +12,8 @@
 I32 = jnp.int32
 MESH = pl.DeviceIdType.MESH
 NORM_EPS = 1e-05
-SCALE = 0.25 * 1.4426950408889634
+LOG2E = 1.4426950408889634
+SCALE = 0.25 * LOG2E
 ROWS = 512
 WIDTH = 256
 PATCH = 1024
@@ -44,7 +45,15 @@
 
 
 def gelu(values):
-    return 0.5 * values * (1.0 + lax.erf(values * 0.7071067811865476))
+    size = jnp.abs(values)
+    under = 1.0 + 0.23164189 * size
+    t = pl.reciprocal(under, approx=True)
+    t = t * (2.0 - under * t)
+    poly = 0.5 * 1.061405429 * t - 0.5 * 1.453152027
+    for factor in (0.5 * 1.421413741, -0.5 * 0.284496736, 0.5 * 0.254829592):
+        poly = poly * t + factor
+    tail = jnp.exp2(values * values * (-0.5 * LOG2E)) * (poly * t)
+    return jnp.maximum(values, 0.0) - size * tail
 
 
 def pipelined(parts, score, finish):
@@ -97,12 +106,9 @@
     att_s,
     catt_out,
     catt_in,
-    zatt_out,
-    zatt_in,
-    own_att,
-    other_att,
-    datt_out,
-    datt_in,
+    att_out,
+    att_in,
+    wide_proj,
     ret_send,
     home,
     ab_send,
@@ -118,10 +124,8 @@
     d_rsem,
     cross_sem,
     catt_sem,
-    za_ssem,
-    za_rsem,
-    da_ssem,
-    da_rsem,
+    at_ssem,
+    at_rsem,
     rt_ssem,
     rt_rsem,
 ):
@@ -208,15 +212,6 @@
     perm = onehot(iota((ROWS, ROWS), 0) == row_of)
     rows_sorted = mm(perm, x_ref[0]).astype(BF)
     xp[...] = rows_sorted
-    code = (index % 4) * PATCH + position
-    high = in_block * (code // 64).astype(BF)
-    low = in_block * (code % 64).astype(BF)
-    lane_of = (kord_of % 2 * 4 + dy_of) * 16 + rank
-    spread = onehot(iota((128, ROWS), 0) == lane_of)
-    tags = mm_nt(high, spread) * 64.0 + mm_nt(low, spread)
-    for block in range(32):
-        tag_send[block] = tags[block : block + 1]
-
     def columns_of(rows):
         padded = jnp.concatenate(
             [rows.astype(F32), jnp.zeros((128 - rows.shape[0], 128), F32)], axis=0
@@ -281,10 +276,19 @@
             acc[rows, group * 256 + 128 : group * 256 + 256] = totals[group][1]
         return carry
 
-    lax.fori_loop(0, 3, own_keys, 0)
+    lax.fori_loop(0, 2, own_keys, 0)
     pl.semaphore_wait(barrier, PEERS)
     pair = copy_to(x_ref.at[0], px, pair_sem.at[0], pair_sem.at[1], pts=other_core)
     pair.start()
+
+    code = (index % 4) * PATCH + position
+    high = in_block * (code // 64).astype(BF)
+    low = in_block * (code % 64).astype(BF)
+    lane_of = (kord_of % 2 * 4 + dy_of) * 16 + rank
+    spread = onehot(iota((128, ROWS), 0) == lane_of)
+    tags = mm_nt(high, spread) * 64.0 + mm_nt(low, spread)
+    for block in range(32):
+        tag_send[block] = tags[block : block + 1]
 
     def tag_copy(block, s, pts):
         return copy_to(tag_send.at[block], tag_recv.at[s], tag_ssem, tag_rsem, pts=pts)
@@ -305,7 +309,6 @@
                 else:
                     tag_copy(block, kord * 4 + dy, place(dy, dz, chip_half)).start()
 
-    lax.fori_loop(3, 4, own_keys, 0)
     for one in loads[1:]:
         one.wait()
     pair.wait()
@@ -335,6 +338,17 @@
         for one in quad_copies:
             one.start()
 
+    def z_copy(kord):
+        rows = pl.ds(kord * 64, 64)
+        return copy_to(
+            recv_a.at[rows], zrows.at[rows], z_ssem.at[kord], z_rsem.at[kord], pts=other_chip
+        )
+
+    def forward(kord):
+        count = 48 if kord == 7 else 64
+        wait_bytes(recv_a.at[pl.ds(kord * 64, count)], ab_recv.at[kord])
+        z_copy(kord).start()
+
     def part_one(part, carry):
         rows = pl.ds(pl.multiple_of(part * 128, 128), 128)
         totals = attend_one(rows, slice(ROWS, PATCH))
@@ -362,7 +376,8 @@
                     pl.when(part < 3)(start)
                 else:
                     start()
-        pl.when(part == 1)(share_tags)
+        pl.when(jnp.logical_or(part == 0, part == 1))(lambda: own_keys(part + 2, None))
+        pl.when(part == 2)(share_tags)
         return carry
 
     lax.fori_loop(0, 4, part_one, 0)
@@ -386,12 +401,6 @@
         return (
             jnp.concatenate(own, axis=1).astype(BF),
             jnp.concatenate(other, axis=1).astype(BF),
-        )
-
-    def z_copy(part):
-        rows = pl.ds(part * 128, 128)
-        return copy_to(
-            recv_a.at[rows], zrows.at[rows], z_ssem.at[part], z_rsem.at[part], pts=other_chip
         )
 
     def d_copy(which, part):
@@ -429,7 +438,7 @@
     end_two = PATCH - jnp.where(full[3], counts[2], counts[3])
     cols = columns_of(sorted_at)
 
-    def build_onehots(t):
+    def build_sort(t):
         lane_row = sorted_at[t : t + 1]
 
         def sort_block(block, carry):
@@ -440,22 +449,21 @@
             return carry
 
         lax.fori_loop(0, 8, sort_block, 0)
-        unsort_m[t * 128 : t * 128 + 128] = onehot(iota((128, 2048), 1) == cols[:, t : t + 1])
-
+
+    for part in range(2):
+        for t in range(8 * part, 8 * part + 8):
+            build_sort(t)
+        for kord in range(4 * part, 4 * part + 4):
+            forward(kord)
     for part in range(4):
-        for t in range(4 * part, 4 * part + 4):
-            build_onehots(t)
-        for kord in (2 * part, 2 * part + 1):
-            count = 48 if kord == 7 else 64
-            wait_bytes(recv_a.at[pl.ds(kord * 64, count)], ab_recv.at[kord])
-        z_copy(part).start()
         rows = slice(part * 128, part * 128 + 128)
         gath[0, rows], dsend[0, rows] = project_two(recv_a[rows])
         d_copy(0, part).start()
 
     def partner_rows(part):
         rows = slice(part * 128, part * 128 + 128)
-        z_copy(part).wait_recv()
+        for kord in (2 * part, 2 * part + 1):
+            z_copy(kord).wait_recv()
         gath[1, rows], dsend[1, rows] = project_two(zrows[rows])
         d_copy(1, part).start()
 
@@ -470,13 +478,11 @@
         gacc[rows, :] = sort_some(rows, (0, 2))
         return carry
 
-    partner_rows(0)
-    partner_rows(1)
     for part in range(4):
         d_copy(0, part).wait_recv()
-    lax.fori_loop(0, 8, sort_own, 0)
-    partner_rows(2)
-    partner_rows(3)
+    lax.fori_loop(0, 8, sort_own, 0, unroll=2)
+    for part in range(4):
+        partner_rows(part)
     for part in range(4):
         d_copy(1, part).wait_recv()
 
@@ -492,8 +498,10 @@
     cross_out[...] = jnp.where(zero_full, gs[0:CROSS], gs[PATCH : PATCH + CROSS])
     cross = copy_to(cross_out, cross_in, cross_sem.at[0], cross_sem.at[1], group=next_grp)
     cross.start()
-    lax.fori_loop(1, 4, sort_rows, 0)
-    lax.fori_loop(5, 8, sort_rows, 0)
+    for block in (1, 2, 3, 5, 6, 7):
+        sort_rows(block, 0)
+    for t in range(16):
+        unsort_m[t * 128 : t * 128 + 128] = onehot(iota((128, 2048), 1) == cols[:, t : t + 1])
     cross.wait()
     first_quad = me < 4
     in_full = jnp.logical_and(first_quad, zero_full)
@@ -505,55 +513,56 @@
 
     head_lane_two = iota((256, 128), 1) // 16
 
-    def attend(query_rows, key_rows, mask):
-        held = []
-
-        def score(head):
-            queries = gs[query_rows, 0:128]
-            masked = jnp.where(head_lane_two == head, queries, jnp.zeros_like(queries))
-            return mm_nt(masked, kpack[key_rows])
-
-        def finish(head, scores):
-            weights = jnp.exp2(scores * SCALE)
-            if mask is not None:
-                weights = jnp.where(mask, weights, 0.0)
-            result = mm(weights.astype(BF), gs[key_rows, 128:256])
-            if held:
-                held[0] = jnp.where(head_lane_two % 4 == head, result, held[0])
-            else:
-                held.append(result)
-
-        pipelined(list(range(4)), score, finish)
-        total = held[0]
-        attended = total / pltpu.roll(total, 64, 1)
-        both = jnp.where(iota((256, 128), 1) < 64, attended, pltpu.roll(attended, 64, 1))
-        att_s[query_rows] = both.astype(BF)
-
-    def attend_full(block, carry):
-        attend(pl.ds(pl.multiple_of(block * 256, 256), 256), slice(0, PATCH), None)
-        return carry
-
-    def attend_rest(block):
+    def full_part(block):
+        return slice(block * 256, block * 256 + 256), slice(0, PATCH), None
+
+    def rest_part(block):
         low_key, high_key = ((0, 512), (0, 768), (256, 1024), (512, 1024))[block]
         size = high_key - low_key
         key_at = iota((1, size), 1) + low_key
         query_at = iota((256, 1), 0) + block * 256
         key_part = (key_at >= end_one).astype(I32) + (key_at >= end_two).astype(I32)
         query_part = (query_at >= end_one).astype(I32) + (query_at >= end_two).astype(I32)
-        attend(
+        return (
             slice(PATCH + block * 256, PATCH + block * 256 + 256),
             slice(PATCH + low_key, PATCH + high_key),
             query_part == key_part,
         )
 
-    attend_full(0, 0)
-    attend_rest(0)
+    def attend(parts):
+        held = {}
+
+        def score(step):
+            query_rows, key_rows, _ = parts[step // 4]
+            queries = gs[query_rows, 0:128]
+            masked = jnp.where(head_lane_two == step % 4, queries, jnp.zeros_like(queries))
+            return mm_nt(masked, kpack[key_rows])
+
+        def finish(step, scores):
+            query_rows, key_rows, mask = parts[step // 4]
+            weights = jnp.exp2(scores * SCALE)
+            if mask is not None:
+                weights = jnp.where(mask, weights, 0.0)
+            total = mm(weights.astype(BF), gs[key_rows, 128:256])
+            if step % 4:
+                total = jnp.where(head_lane_two % 4 == step % 4, total, held[step // 4])
+            held[step // 4] = total
+            if step % 4 == 3:
+                attended = total / pltpu.roll(total, 64, 1)
+                both = jnp.where(
+                    iota((256, 128), 1) < 64, attended, pltpu.roll(attended, 64, 1)
+                )
+                att_s[query_rows] = both.astype(BF)
+
+        pipelined(list(range(4 * len(parts))), score, finish)
+
+    attend([full_part(0), rest_part(0)])
     catt_out[...] = jnp.where(zero_full, att_s[0:CROSS], att_s[PATCH : PATCH + CROSS])
     cross_back = copy_to(catt_out, catt_in, catt_sem.at[0], catt_sem.at[1], group=last_grp)
     cross_back.start()
-    lax.fori_loop(1, 4, attend_full, 0)
-    for block in range(1, 4):
-        attend_rest(block)
+    attend([full_part(1), full_part(2)])
+    attend([full_part(3), rest_part(1)])
+    attend([rest_part(2), rest_part(3)])
     cross_back.wait()
     att_s[0:CROSS] = jnp.where(in_full, catt_in[...], att_s[0:CROSS])
     att_s[PATCH : PATCH + CROSS] = jnp.where(
@@ -563,50 +572,53 @@
     def unsorted(rel, at, size):
         return mm(unsort_m[rel * 512 + at : rel * 512 + at + size], att_s[...])
 
-    def za_copy(part):
+    def att_copy(rel, part):
         rows = pl.ds(part * 128, 128)
+        sem = rel * 2 + part
         return copy_to(
-            zatt_out.at[rows], zatt_in.at[rows], za_ssem.at[part], za_rsem.at[part], pts=other_chip
-        )
-
-    def da_copy(part):
-        rows = pl.ds(part * 128, 128)
-        return copy_to(
-            datt_out.at[rows], datt_in.at[rows], da_ssem.at[part], da_rsem.at[part], pts=other_core
-        )
-
-    low_lane_two = iota((256, 128), 1) < 64
+            att_out.at[rel, rows],
+            att_in.at[rel, rows],
+            at_ssem.at[sem],
+            at_rsem.at[sem],
+            pts=(None, other_chip, other_core, diagonal)[rel],
+        )
+
     for part in range(2):
-        rows = slice(part * 256, part * 256 + 256)
-        zatt_out[rows] = jnp.where(
-            low_lane_two, unsorted(1, part * 256, 256), unsorted(3, part * 256, 256)
-        ).astype(BF)
-        za_copy(2 * part).start()
-        za_copy(2 * part + 1).start()
-    other_att[...] = unsorted(2, 0, ROWS)
-    own_att[...] = unsorted(0, 0, ROWS).astype(BF)
+        rows = slice(part * 128, part * 128 + 128)
+        for rel in (3, 1, 2):
+            result = unsorted(rel, part * 256, 256)
+            att_out[rel, rows] = jnp.where(low_lane, result[:128], result[128:]).astype(BF)
+            att_copy(rel, part).start()
+    for part in range(2):
+        rows = slice(part * 128, part * 128 + 128)
+        result = unsorted(0, part * 256, 256)
+        att_in[0, rows] = jnp.where(low_lane, result[:128], result[128:]).astype(BF)
 
     def proj_rows(chip_half, chip_core):
         at = pl.multiple_of((chip_half * 2 + chip_core) * 64, 64)
         return proj_ref[1, pl.ds(at, 64), :]
 
-    weights_a = jnp.concatenate([proj_rows(half, core), proj_rows(1 - half, core)], axis=0)
-    weights_b = jnp.concatenate([proj_rows(half, 1 - core), proj_rows(1 - half, 1 - core)], axis=0)
-
-    def regroup(part):
+    zeros = jnp.zeros((64, WIDTH), BF)
+    owners = ((half, core), (1 - half, core), (half, 1 - core), (1 - half, 1 - core))
+    for rel, (chip_half, chip_core) in enumerate(owners):
+        low, high = rel * 128, rel * 128 + 64
+        weights = proj_rows(chip_half, chip_core)
+        wide_proj[0, low : low + 64] = weights
+        wide_proj[0, high : high + 64] = zeros
+        wide_proj[1, low : low + 64] = zeros
+        wide_proj[1, high : high + 64] = weights
+
+    def part_two(part, carry):
         rows = pl.ds(pl.multiple_of(part * 128, 128), 128)
-        za_copy(part).wait_recv()
-        arrived = zatt_in[rows, :].astype(F32)
-        datt_out[rows, :] = jnp.where(low_lane, other_att[rows, :], arrived).astype(BF)
-        da_copy(part).start()
-        own_att[rows, :] = jnp.where(
-            low_lane, own_att[rows, :], pltpu.roll(arrived, 64, 1).astype(BF)
-        )
-
-    def part_two(part):
-        rows = pl.ds(pl.multiple_of(part * 128, 128), 128)
-        da_copy(part).wait_recv()
-        out_rows = mm(own_att[rows, :], weights_a) + mm(datt_in[rows, :], weights_b)
+        packed = pl.ds(pl.multiple_of(part // 2 * 128, 128), 128)
+
+        def arrive():
+            for rel in range(1, 4):
+                att_copy(rel, part // 2).wait_recv()
+
+        pl.when(part % 2 == 0)(arrive)
+        attended = jnp.concatenate([att_in[rel, packed, :] for rel in range(4)], axis=1)
+        out_rows = mm(attended, wide_proj[part % 2])
         mixed = recv_a[rows, :].astype(F32) + (out_rows + outb_ref[1, 0:1])
         ret_send[rows, :] = feed_forward(mixed.astype(BF), 1)
         first = (3 - part) // 3
@@ -635,12 +647,9 @@
                 else:
                     start()
 
-    def return_step(step, carry):
-        pl.when(step < 4)(lambda: regroup(step))
-        pl.when(step > 0)(lambda: part_two(step - 1))
         return carry
 
-    lax.fori_loop(0, 5, return_step, 0)
+    lax.fori_loop(0, 4, part_two, 0)
     row_cols = columns_of(
         jnp.concatenate([row_of[:, t * 128 : t * 128 + 128] for t in range(4)], axis=0)
     )
@@ -656,14 +665,14 @@
     for one in quad_copies:
         one.wait_send()
     wait_bytes(send_a.at[pl.ds(0, 496)], ab_send)
-    for part in range(4):
-        z_copy(part).wait_send()
+    for kord in range(8):
+        z_copy(kord).wait_send()
     for which in range(2):
         for part in range(4):
             d_copy(which, part).wait_send()
-    for part in range(4):
-        za_copy(part).wait_send()
-        da_copy(part).wait_send()
+    for rel in range(1, 4):
+        for part in range(2):
+            att_copy(rel, part).wait_send()
     wait_bytes(ret_send.at[pl.ds(0, 496)], rt_ssem)
 
 
@@ -683,7 +692,6 @@
     vmem = pl.BlockSpec(memory_space=pltpu.VMEM)
     sems = pltpu.SemaphoreType.DMA
     rows_buffer = pltpu.VMEM((ROWS, WIDTH), BF)
-    half_buffer = pltpu.VMEM((ROWS, 128), BF)
     any_space = pl.BlockSpec(memory_space=pl.ANY)
     scratch = [
         pltpu.VMEM((2, WIDTH, 3 * WIDTH), BF),
@@ -716,12 +724,9 @@
         pltpu.VMEM((2 * PATCH, 128), BF),
         pltpu.VMEM((CROSS, 128), BF),
         pltpu.VMEM((CROSS, 128), BF),
-        half_buffer,
-        half_buffer,
-        half_buffer,
-        pltpu.VMEM((ROWS, 128), F32),
-        half_buffer,
-        half_buffer,
+        pltpu.VMEM((4, 256, 128), BF),
+        pltpu.VMEM((4, 256, 128), BF),
+        pltpu.VMEM((2, 2 * WIDTH, WIDTH), BF),
         rows_buffer,
         rows_buffer,
         sems,
@@ -731,16 +736,14 @@
         sems((4,)),
         sems((4,)),
         sems((2,)),
-        sems((4,)),
-        sems((4,)),
+        sems((8,)),
+        sems((8,)),
         sems((8,)),
         sems((8,)),
         sems((2,)),
         sems((2,)),
-        sems((4,)),
-        sems((4,)),
-        sems((4,)),
-        sems((4,)),
+        sems((8,)),
+        sems((8,)),
         sems,
         sems((8,)),
     ]

time: 86.8 us -> 83.5 us (0.962)
  Pallas kernels: 84.9 us -> 81.7 us
    pallas_call x1, Pallas kernels: 84.9 us -> 81.7 us  [on_device(): pl.pallas_call(kernel, out_shape=jax.ShapeDtypeStruct((1, ROWS, WIDTH), B...]
where the time goes in v3:
time: 83.5 us; the launch traced here: 83.4 us
  Pallas kernels  81.7 us (98%)
  local copies, waits for them, and re-layouts  1.67 us (2%)
    pallas_call x1, Pallas kernels, on_device(): pl.pallas_call(kernel, out_shape=jax.ShapeDtypeStruct((1, ROWS, WIDTH), B...  81.7 us
    unnamed x1, local copies, waits for them, and re-layouts  1.67 us

profile of v3, /device:TPU:1, one launch (start us, length us, event | category | flops | bytes accessed | tf_op | source)
XLA Modules:
  0.0 83.4 jit_solution(500899383622152948)
XLA Ops:
  0.0 81.7 %shard_map.100 = bf16[1,512,256]{2,1,0:T(8,128)(2,1)} custom-call(bf16[1,512,256]{2,1,0:T(8,128)(2,1)} %x_ref.1, s32[1,512]{1,0:T(1,128)} %slot_ref.1, f32[2,2,256]{2,1,0:T(2,128)} %gain_ref.1, f32[2,2,256]{2,1,0:T(2,128)} %shift_ref.1, bf16[2,256,768]{2,1,0:T(8,128)(2,1)} %qkv_any.1, bf16[2,256,256]{2,1,0:T(8,128)(2,1)} %proj_any.1, ...), custom_call_target="tpu_custom_call" | custom-call | tf_op jit(solution)/shard_map/pallas_call | solution.py:750
  81.7 1.7 %copy.12 = bf16[1,512,256]{2,1,0:T(8,128)(2,1)} copy(bf16[1,512,256]{2,1,0:T(8,128)(2,1)} %shard_map.100) | data formatting | bytes 524288

commit v4 on v3

--- a/solution.py
+++ b/solution.py
@@ -276,7 +276,7 @@
             acc[rows, group * 256 + 128 : group * 256 + 256] = totals[group][1]
         return carry
 
-    lax.fori_loop(0, 2, own_keys, 0)
+    lax.fori_loop(0, 3, own_keys, 0)
     pl.semaphore_wait(barrier, PEERS)
     pair = copy_to(x_ref.at[0], px, pair_sem.at[0], pair_sem.at[1], pts=other_core)
     pair.start()
@@ -309,6 +309,7 @@
                 else:
                     tag_copy(block, kord * 4 + dy, place(dy, dz, chip_half)).start()
 
+    lax.fori_loop(3, 4, own_keys, 0)
     for one in loads[1:]:
         one.wait()
     pair.wait()
@@ -376,7 +377,6 @@
                     pl.when(part < 3)(start)
                 else:
                     start()
-        pl.when(jnp.logical_or(part == 0, part == 1))(lambda: own_keys(part + 2, None))
         pl.when(part == 2)(share_tags)
         return carry
 

time: 83.5 us -> 82.4 us (0.987); the launches traced: 83.4 us -> 81.4 us
  Pallas kernels: 81.7 us -> 79.7 us
    pallas_call x1, Pallas kernels: 81.7 us -> 79.7 us  [on_device(): pl.pallas_call(kernel, out_shape=jax.ShapeDtypeStruct((1, ROWS, WIDTH), B...]
where the time goes in v4:
time: 82.4 us; the launch traced here: 81.4 us
  Pallas kernels  79.7 us (97%)
  local copies, waits for them, and re-layouts  1.67 us (2%)
    pallas_call x1, Pallas kernels, on_device(): pl.pallas_call(kernel, out_shape=jax.ShapeDtypeStruct((1, ROWS, WIDTH), B...  79.7 us
    unnamed x1, local copies, waits for them, and re-layouts  1.67 us

profile of v4, /device:TPU:1, one launch (start us, length us, event | category | flops | bytes accessed | tf_op | source)
XLA Modules:
  0.0 81.4 jit_solution(3135007982901711806)
XLA Ops:
  0.0 79.7 %shard_map.100 = bf16[1,512,256]{2,1,0:T(8,128)(2,1)} custom-call(bf16[1,512,256]{2,1,0:T(8,128)(2,1)} %x_ref.1, s32[1,512]{1,0:T(1,128)} %slot_ref.1, f32[2,2,256]{2,1,0:T(2,128)} %gain_ref.1, f32[2,2,256]{2,1,0:T(2,128)} %shift_ref.1, bf16[2,256,768]{2,1,0:T(8,128)(2,1)} %qkv_any.1, bf16[2,256,256]{2,1,0:T(8,128)(2,1)} %proj_any.1, ...), custom_call_target="tpu_custom_call" | custom-call | tf_op jit(solution)/shard_map/pallas_call | solution.py:750
  79.7 1.7 %copy.12 = bf16[1,512,256]{2,1,0:T(8,128)(2,1)} copy(bf16[1,512,256]{2,1,0:T(8,128)(2,1)} %shard_map.100) | data formatting | bytes 524288

commit v5 on v4

--- a/solution.py
+++ b/solution.py
@@ -377,7 +377,7 @@
                     pl.when(part < 3)(start)
                 else:
                     start()
-        pl.when(part == 2)(share_tags)
+        pl.when(part == 1)(share_tags)
         return carry
 
     lax.fori_loop(0, 4, part_one, 0)

time: 82.4 us -> 82.4 us (level)
  no operation moved by 1% of the time
where the time goes in v5:
time: 82.4 us; the launch traced here: 81.6 us
  Pallas kernels  80 us (97%)
  local copies, waits for them, and re-layouts  1.67 us (2%)
    pallas_call x1, Pallas kernels, on_device(): pl.pallas_call(kernel, out_shape=jax.ShapeDtypeStruct((1, ROWS, WIDTH), B...  80 us
    unnamed x1, local copies, waits for them, and re-layouts  1.67 us

profile of v5, /device:TPU:1, one launch (start us, length us, event | category | flops | bytes accessed | tf_op | source)
XLA Modules:
  0.0 81.6 jit_solution(17057129128553888430)
XLA Ops:
  0.0 80.0 %shard_map.100 = bf16[1,512,256]{2,1,0:T(8,128)(2,1)} custom-call(bf16[1,512,256]{2,1,0:T(8,128)(2,1)} %x_ref.1, s32[1,512]{1,0:T(1,128)} %slot_ref.1, f32[2,2,256]{2,1,0:T(2,128)} %gain_ref.1, f32[2,2,256]{2,1,0:T(2,128)} %shift_ref.1, bf16[2,256,768]{2,1,0:T(8,128)(2,1)} %qkv_any.1, bf16[2,256,256]{2,1,0:T(8,128)(2,1)} %proj_any.1, ...), custom_call_target="tpu_custom_call" | custom-call | tf_op jit(solution)/shard_map/pallas_call | solution.py:750
  80.0 1.7 %copy.12 = bf16[1,512,256]{2,1,0:T(8,128)(2,1)} copy(bf16[1,512,256]{2,1,0:T(8,128)(2,1)} %shard_map.100) | data formatting | bytes 524288
